TPU v7x, 32 devices: a whole 2x2x4 slice. The times are simulated.
32 devices in a mesh: depth: 4 (over y, x), row: 2 (over core), col: 4 (over z).
Axes of the slice: x: 2, y: 2, z: 4, core: 2. Of those that a mesh axis runs over, the one named last changes fastest.
Arguments:
- tokens: bfloat16 [512, 6144], P(('depth', 'row'), 'col'), may hold values from -6 to 6
- grad_out: bfloat16 [512, 6144], P(('depth', 'row'), 'col'), may hold values from -6 to 6
- w_up: bfloat16 [6144, 24576], P(('col', 'depth'), 'row'), may hold values from -0.078125 to 0.078125
- w_down: bfloat16 [6144, 24576], P(('col', 'depth'), 'row'), may hold values from -0.0390625 to 0.0390625
Outputs:
- grad_in: bfloat16 [512, 6144], P(('depth', 'row'), 'col')
- grad_up: bfloat16 [6144, 24576], P(('col', 'depth'), 'row')
- grad_down: bfloat16 [6144, 24576], P(('col', 'depth'), 'row')
All inputs are finite; a program needn't handle non-finite values.
Results may differ from a plain program's by a relative error of at most 0.03.
Values may be sent and summed in bfloat16 or wider, within the bound.
A program may use at most 256 MiB of HBM per device.

v0:
```python
import math

import jax
import jax.numpy as jnp
from jax import lax
from jax.sharding import PartitionSpec as P


def gelu_parts(hidden):
    coeff = math.sqrt(2.0 / math.pi)
    cube = hidden * hidden * hidden
    slope_in = jnp.tanh(coeff * (hidden + 0.044715 * cube))
    value = 0.5 * hidden * (1.0 + slope_in)
    slope = 0.5 * (1.0 + slope_in) + 0.5 * hidden * (1.0 - slope_in * slope_in) * coeff * (
        1.0 + 3.0 * 0.044715 * hidden * hidden
    )
    return (value, slope)


def body(tokens, grad_out, w_up, w_down):
    depth_pos = lax.axis_index("depth")
    up_block, down_block = (
        lax.all_gather(w_up, "depth", axis=0, tiled=True),
        lax.all_gather(w_down, "depth", axis=0, tiled=True),
    )
    x_rows, dy_rows = (
        lax.all_gather(tokens, ("depth", "row"), axis=0, tiled=True),
        lax.all_gather(grad_out, ("depth", "row"), axis=0, tiled=True),
    )
    own_count = x_rows.shape[0] // lax.axis_size("depth")
    own_start = depth_pos * own_count
    x_own = lax.dynamic_slice_in_dim(x_rows, own_start, own_count, 0)
    dy_own = lax.dynamic_slice_in_dim(dy_rows, own_start, own_count, 0)
    narrow = w_up.shape[0]
    dy_narrow = lax.dynamic_slice_in_dim(dy_rows, depth_pos * narrow, narrow, 1)
    pre_part = jnp.dot(x_rows, up_block, preferred_element_type=jnp.float32)
    grad_part = jnp.dot(dy_own, down_block, preferred_element_type=jnp.float32)
    hidden_pre, act_grad = (
        lax.psum(pre_part.astype(jnp.bfloat16), "col").astype(jnp.float32),
        lax.psum(grad_part.astype(jnp.bfloat16), "col").astype(jnp.float32),
    )
    act_value, slope = gelu_parts(hidden_pre)
    act_rows = act_value.astype(jnp.bfloat16)
    slope_own = lax.dynamic_slice_in_dim(slope, own_start, own_count, 0)
    hidden_grad = (act_grad * slope_own).astype(jnp.bfloat16)
    grad_up = lax.psum_scatter(
        lax.dot_general(
            x_own, hidden_grad, (((0,), (0,)), ((), ())), preferred_element_type=jnp.float32
        ).astype(jnp.bfloat16),
        "depth",
        scatter_dimension=0,
        tiled=True,
    )
    grad_in = lax.psum_scatter(
        lax.dot_general(
            hidden_grad, up_block, (((1,), (1,)), ((), ())), preferred_element_type=jnp.float32
        ).astype(jnp.bfloat16),
        "row",
        scatter_dimension=0,
        tiled=True,
    )
    grad_down = lax.dot_general(
        dy_narrow, act_rows, (((0,), (0,)), ((), ())), preferred_element_type=jnp.float32
    ).astype(jnp.bfloat16)
    return (grad_in, grad_up, grad_down)


def solution(mesh):
    placed = (
        P(("depth", "row"), "col"),
        P(("depth", "row"), "col"),
        P(("col", "depth"), "row"),
        P(("col", "depth"), "row"),
    )
    return jax.shard_map(
        body,
        mesh=mesh,
        in_specs=placed,
        out_specs=(
            P(("depth", "row"), "col"),
            P(("col", "depth"), "row"),
            P(("col", "depth"), "row"),
        ),
        check_vma=False,
    )
```

profile of v0, /device:TPU:0, one launch (start us, length us, event | category | flops | bytes accessed | tf_op | source)
XLA Modules:
  0.0 1694.4 jit_solution(15262524113560906517)
XLA Ops:
  7.2 0.7 all-gather.9.cloned.1.call-update
  7.9 0.0 all-gather.11.cloned.1.call-start
  7.9 0.7 all-gather.11.cloned.1.call-update
  8.6 0.0 all-gather.5.cloned.1.call-start
  8.7 0.7 all-gather.5.cloned.1.call-update
  9.4 0.0 all-gather.7.cloned.1.call-start
  9.4 0.5 all-gather.7.cloned.1.call-update
  10.0 0.0 all-reduce.3.cloned.1.call-start
  10.0 28.3 %all-gather.9.cloned.1.call-done = bf16[512,1536]{1,0:T(8,128)(2,1)} async-done(((bf16[64,1536]{1,0:T(8,128)(2,1)}), bf16[512,1536]{1,0:T(8,128)(2,1)}) %all-gather.9.cloned.1.call-update) | async-done | bytes 1572880 | tf_op jit(solution)/shard_map/all_gather | solution.py:27
  38.3 334.9 %all-gather.11.cloned.1.call-done = bf16[1536,12288]{1,0:T(8,128)(2,1)} async-done(((bf16[384,12288]{1,0:T(8,128)(2,1)}), bf16[1536,12288]{1,0:T(8,128)(2,1)}) %all-gather.11.cloned.1.call-update) | async-done | bytes 37748752 | tf_op jit(solution)/shard_map/all_gather | solution.py:23
  373.2 27.1 %convolution_convert_fusion.1 = bf16[512,12288]{1,0:T(8,128)(2,1)} fusion(bf16[512,1536]{1,0:T(8,128)(2,1)} %all-gather.9.cloned.1.call-done, bf16[1536,12288]{1,0:T(8,128)(2,1)} %all-gather.11.cloned.1.call-done), kind=kOutput, calls=%fused_computation.7 | convolution fusion | flops 19333644288 | bytes 51904512 | tf_op jit(solution)/shard_map/dot_general | solution.py:36
  400.3 0.6 all-gather.5.cloned.1.call-done
  400.8 334.8 %all-gather.7.cloned.1.call-done = bf16[1536,12288]{1,0:T(8,128)(2,1)} async-done(((bf16[384,12288]{1,0:T(8,128)(2,1)}), bf16[1536,12288]{1,0:T(8,128)(2,1)}) %all-gather.7.cloned.1.call-update) | async-done | bytes 37748752 | tf_op jit(solution)/shard_map/all_gather | solution.py:24
  735.6 16.2 convolution_convert_fusion.3
  751.8 0.2 reduce-scatter.3.cloned.1.call-start
  752.0 528.2 %all-reduce.3.cloned.1.call-done = (bf16[512,12288]{1,0:T(8,128)(2,1)}, bf16[128,12288]{1,0:T(8,128)(2,1)}) async-done(((bf16[512,12288]{1,0:T(8,128)(2,1)}, bf16[128,12288]{1,0:T(8,128)(2,1)}), (bf16[512,12288]{1,0:T(8,128)(2,1)}, bf16[128,12288]{1,0:T(8,128)(2,1)})) %all-reduce.3.cloned.1.call-update) | async-done | bytes 15728656 | tf_op jit(solution)/shard_map/psum | solution.py:39
  1280.3 31.5 %fusion.3 = (f32[512,12288]{1,0:T(8,128)}, f32[512,12288]{1,0:T(8,128)}, f32[512,12288]{1,0:T(8,128)}) fusion(bf16[512,12288]{1,0:T(8,128)(2,1)} %get-tuple-element.3), kind=kLoop, calls=%fused_computation.5 | loop fusion | flops 50331648 | bytes 88080384 | tf_op jit(solution)/shard_map/tanh | solution.py:12
  1311.8 8.9 convert_element_type.30
  1320.6 9.6 fusion.8
  1330.2 18.5 %convolution_convert_fusion.4 = bf16[128,1536]{1,0:T(8,128)(2,1)} fusion(bf16[128,12288]{1,0:T(8,128)(2,1)S(1)} %fusion.8, bf16[1536,12288]{1,0:T(8,128)(2,1)} %all-gather.11.cloned.1.call-done), kind=kOutput, calls=%fused_computation.23 | convolution fusion | flops 4832034816 | bytes 41287680 | tf_op jit(solution)/shard_map/dot_general | solution.py:55
  1348.7 0.3 reduce-scatter.5.cloned.1.call-start
  1349.0 17.1 %convolution_convert_fusion = bf16[1536,12288]{1,0:T(8,128)(2,1)} fusion(bf16[128,12288]{1,0:T(8,128)(2,1)S(1)} %fusion.8, bf16[512,1536]{1,0:T(8,128)(2,1)} %all-gather.9.cloned.1.call-done, s32[]{:T(128)S(6)} %select_n.8), kind=kOutput, calls=%fused_computation | convolution fusion | flops 4850712576 | bytes 41287684 | tf_op jit(solution)/shard_map/dot_general | solution.py:47
  1366.1 16.2 convolution_convert_fusion.2
  1382.3 305.3 %reduce-scatter.5.cloned.1.call-done = bf16[384,12288]{1,0:T(8,128)(2,1)} async-done(((bf16[1536,12288]{1,0:T(8,128)(2,1)}), bf16[384,12288]{1,0:T(8,128)(2,1)}) %reduce-scatter.5.cloned.1.call-update) | async-done | bytes 9437200 | tf_op jit(solution)/shard_map/reduce_scatter | solution.py:46
  (9 shorter events, 0.1 us)
Async XLA Ops:
  7.2 31.1 %all-gather.9.cloned.1.call-start = ((), (), s32[]{:S(2)}) async-start(), calls=%async_computation.4 | async-start | bytes 1769472 | tf_op jit(solution)/shard_map/all_gather | solution.py:27
  7.9 365.3 %all-gather.11.cloned.1.call-start = ((), (), s32[]{:S(2)}) async-start(), calls=%async_computation.5 | async-start | bytes 47185920 | tf_op jit(solution)/shard_map/all_gather | solution.py:23
  8.6 392.2 %all-gather.5.cloned.1.call-start = ((), (), s32[]{:S(2)}) async-start(), calls=%async_computation.2 | async-start | bytes 1769472 | tf_op jit(solution)/shard_map/all_gather | solution.py:28
  9.4 726.2 %all-gather.7.cloned.1.call-start = ((), (), s32[]{:S(2)}) async-start(), calls=%async_computation.3 | async-start | bytes 47185920 | tf_op jit(solution)/shard_map/all_gather | solution.py:24
  10.0 1270.3 %all-reduce.3.cloned.1.call-start = ((), (), s32[]{:S(2)}) async-start(), calls=%async_computation.8 | async-start | bytes 31457280 | tf_op jit(solution)/shard_map/psum | solution.py:39
  751.8 630.5 %reduce-scatter.3.cloned.1.call-start = ((), (), s32[]{:S(2)}) async-start(), calls=%async_computation.6 | async-start | bytes 589824 | tf_op jit(solution)/shard_map/reduce_scatter | solution.py:54
  1280.3 31.5 %copy-start = (bf16[512,12288]{1,0:T(8,128)(2,1)S(1)}, bf16[512,12288]{1,0:T(8,128)(2,1)}, u32[]{:S(2)}) copy-start(bf16[512,12288]{1,0:T(8,128)(2,1)} %get-tuple-element.3) | copy-start | bytes 37748740
  1311.8 8.9 copy-start.1
  1348.7 338.8 %reduce-scatter.5.cloned.1.call-start = ((), (), s32[]{:S(2)}) async-start(), calls=%async_computation.7 | async-start | bytes 47185920 | tf_op jit(solution)/shard_map/reduce_scatter | solution.py:46
Sparse Core Ops, SparseCore 0:
  9.9 28.3 all-gather.8
  40.2 332.9 all-gather.10
  375.1 25.6 all-gather.4
  402.6 332.9 all-gather.6
  751.9 528.2 all-reduce.2
  1348.9 6.5 reduce-scatter.2
  1366.2 321.3 reduce-scatter.4
where the time goes:
time: 1690 us
  waiting for transfers between devices  1530 us (91%)
  matrix products  95 us (6%)
  other arithmetic  50 us (3%)
    psum x1, waiting for transfers between devices, body(): lax.psum(pre_part.astype(jnp.bfloat16), 'col').astype(jnp.float32)  528 us
    all_gather x1, waiting for transfers between devices, body(): lax.all_gather(w_up, 'depth', axis=0, tiled=True)  335 us
    all_gather x1, waiting for transfers between devices, body(): lax.all_gather(w_down, 'depth', axis=0, tiled=True)  335 us
    reduce_scatter x1, waiting for transfers between devices, body(): lax.psum_scatter(lax.dot_general(x_own, hidden_grad, (((0,), (0,)), ((),...  305 us
  transfers between devices with their start and end apart: 7, of which 6 were waited for; matrix products, arithmetic and copies ran while one was open for 4% of the time, Pallas kernels for 0%

commit v1 on v0

v1 whole, which is shorter than its diff:
```python
import math

import jax
import jax.numpy as jnp
from jax import lax
from jax.sharding import PartitionSpec as P


def gelu_parts(hidden):
    coeff = math.sqrt(2.0 / math.pi)
    cube = hidden * hidden * hidden
    slope_in = jnp.tanh(coeff * (hidden + 0.044715 * cube))
    value = 0.5 * hidden * (1.0 + slope_in)
    slope = 0.5 * (1.0 + slope_in) + 0.5 * hidden * (1.0 - slope_in * slope_in) * coeff * (
        1.0 + 3.0 * 0.044715 * hidden * hidden
    )
    return (value, slope)


def line_reduce_scatter(parts, axis, name):
    count = lax.axis_size(name)
    here = lax.axis_index(name)

    def piece(index):
        return lax.dynamic_index_in_dim(
            parts, jnp.clip(index, 0, count - 1), axis, keepdims=False
        )

    up, down = None, None
    for step in range(1, count):
        send_up = piece(here + count - step)
        send_down = piece(here + step - count)
        if up is not None:
            send_up = send_up + up
            send_down = send_down + down
        up = lax.ppermute(send_up, name, [(i, i + 1) for i in range(step)])
        down = lax.ppermute(
            send_down, name, [(i, i - 1) for i in range(count - step, count)]
        )
    own = piece(here).astype(jnp.float32)
    return own + up.astype(jnp.float32) + down.astype(jnp.float32)


def line_all_gather(block, axis, name):
    count = lax.axis_size(name)
    here = lax.axis_index(name)
    ups, downs = [], []
    up = down = block
    for step in range(1, count):
        up = lax.ppermute(up, name, [(i, i + 1) for i in range(step - 1, count - 1)])
        down = lax.ppermute(down, name, [(i, i - 1) for i in range(1, count - step + 1)])
        ups.append(up)
        downs.append(down)
    shape = block.shape[:axis] + (count,) + block.shape[axis:]
    whole = lax.dynamic_update_index_in_dim(
        jnp.zeros(shape, block.dtype), block, here, axis
    )
    for step in range(1, count):
        arrived = jnp.where(here >= step, ups[step - 1], downs[count - step - 1])
        whole = lax.dynamic_update_index_in_dim(
            whole, arrived, lax.rem(here - step + count, count), axis
        )
    return whole


def body(tokens, grad_out, w_up, w_down):
    n_depth, n_row, n_col = (lax.axis_size(a) for a in ("depth", "row", "col"))
    rows, part = tokens.shape
    narrow, hidden = w_up.shape
    group = n_depth * n_row
    total = group * rows
    bunch = total // (n_depth * n_col)
    far = hidden // 4 // 128 * 128
    near = hidden - far
    bf16, f32 = jnp.bfloat16, jnp.float32

    both = jnp.stack([tokens, grad_out]).reshape(2, rows, n_depth, narrow)
    both = jnp.transpose(both, (2, 0, 1, 3))
    both = jnp.broadcast_to(both[:, None], (n_depth, n_row, 2, rows, narrow))
    both = both.reshape(group, 2, rows, narrow)
    both = lax.all_to_all(both, ("depth", "row"), 0, 0, tiled=True)
    x_cols = both[:, 0].reshape(total, narrow)
    dy_cols = both[:, 1].reshape(total, narrow)

    def product(left, right):
        return jnp.dot(left, right, preferred_element_type=f32).astype(bf16)

    def outer(left, right):
        return lax.dot_general(
            left, right, (((0,), (0,)), ((), ())), preferred_element_type=f32
        ).astype(bf16)

    pre_near = product(x_cols, w_up[:, :near])
    pre_near = lax.psum_scatter(pre_near, "depth", scatter_dimension=0, tiled=True)
    far_terms = jnp.concatenate(
        [product(x_cols, w_up[:, near:]), product(dy_cols, w_down[:, near:])], axis=1
    )
    far_terms = line_reduce_scatter(
        far_terms.reshape(n_depth, n_col, bunch, 2 * far), 1, "col"
    ).astype(bf16)
    grad_near = product(dy_cols, w_down[:, :near])
    pre_near, grad_near = lax.optimization_barrier((pre_near, grad_near))
    grad_near = lax.psum_scatter(grad_near, "depth", scatter_dimension=0, tiled=True)
    pre_near = line_reduce_scatter(pre_near.reshape(n_col, bunch, near), 0, "col")
    far_sum = lax.psum_scatter(
        far_terms.reshape(n_depth * bunch, 2 * far), "depth", scatter_dimension=0, tiled=True
    ).astype(f32)
    grad_near = line_reduce_scatter(grad_near.reshape(n_col, bunch, near), 0, "col")

    far_value, far_slope = gelu_parts(far_sum[:, :far])
    far_pair = jnp.concatenate(
        [far_value.astype(bf16), (far_sum[:, far:] * far_slope).astype(bf16)], axis=1
    )
    near_value, near_slope = gelu_parts(pre_near)
    act_near = near_value.astype(bf16)
    hid_near = (grad_near * near_slope).astype(bf16)

    far_pair = lax.all_gather(far_pair, "depth", axis=0, tiled=False)
    act_near = line_all_gather(act_near, 0, "col").reshape(n_col * bunch, near)
    act_near = lax.all_gather(act_near, "depth", axis=0, tiled=True)
    hid_near = line_all_gather(hid_near, 0, "col").reshape(n_col * bunch, near)
    act_near, hid_near = lax.optimization_barrier((act_near, hid_near))
    hid_near = lax.all_gather(hid_near, "depth", axis=0, tiled=True)
    far_pair = line_all_gather(far_pair, 1, "col").reshape(total, 2 * far)

    grad_down = jnp.concatenate(
        [outer(dy_cols, act_near), outer(dy_cols, far_pair[:, :far])], axis=1
    )
    grad_up = jnp.concatenate(
        [outer(x_cols, hid_near), outer(x_cols, far_pair[:, far:])], axis=1
    )

    def back(left, right):
        return lax.dot_general(
            left, right, (((1,), (1,)), ((), ())), preferred_element_type=f32
        )

    grad_in = back(hid_near, w_up[:, :near]) + back(far_pair[:, far:], w_up[:, near:])
    grad_in = grad_in.astype(bf16).reshape(group, rows, narrow)
    grad_in = lax.all_to_all(grad_in, ("depth", "row"), 0, 0, tiled=True)
    grad_in = grad_in.reshape(n_depth, n_row, rows, narrow).astype(f32).sum(axis=1)
    grad_in = jnp.transpose(grad_in, (1, 0, 2)).reshape(rows, part).astype(bf16)
    return (grad_in, grad_up, grad_down)


def solution(mesh):
    placed = (
        P(("depth", "row"), "col"),
        P(("depth", "row"), "col"),
        P(("col", "depth"), "row"),
        P(("col", "depth"), "row"),
    )
    return jax.shard_map(
        body,
        mesh=mesh,
        in_specs=placed,
        out_specs=(
            P(("depth", "row"), "col"),
            P(("col", "depth"), "row"),
            P(("col", "depth"), "row"),
        ),
        check_vma=False,
    )
```

time: 1690 us -> 690 us (0.41)
  waiting for transfers between devices: 1530 us -> 466 us
  starting transfers between devices: 0.67 us -> 81.6 us
  matrix products: 95 us -> 59.7 us
  blocking collectives: 0 us -> 17.5 us
    all_gather x4 -> x3, waiting for transfers between devices: 699 us -> 44.6 us  [the longest x1 33.2 us: body(): far_pair = lax.all_gather(far_pair, 'depth', axis=0, tiled=False)]
    psum x1 -> x0, waiting for transfers between devices: 528 us -> none  [body(): lax.psum(pre_part.astype(jnp.bfloat16), 'col').astype(jnp.float32)]
    ppermute x0 -> x36, waiting for transfers between devices: none -> 338 us  [the longest x9 186 us: line_all_gather(): lax.ppermute(down, name, [(i, i - 1) for i in range(1, count - step + 1)])]
    reduce_scatter x2 -> x3, waiting for transfers between devices: 305 us -> 84.1 us  [the longest x1 84.1 us: body(): lax.psum_scatter(pre_near, 'depth', scatter_dimension=0, tiled=True)]
    ppermute x0 -> x36, starting transfers between devices: none -> 78 us  [the longest x9 31.7 us: line_reduce_scatter(): up = lax.ppermute(send_up, name, [(i, i + 1) for i in range(step)])]
    dot_general x5 -> x10, matrix products: 95 us -> 59.7 us  [the longest x4 29.5 us: product(): return jnp.dot(left, right, preferred_element_type=f32).astype(bf16)]
    tanh x1 -> x0, other arithmetic: 31.5 us -> none  [gelu_parts(): slope_in = jnp.tanh(coeff * (hidden + 0.044715 * cube))]
    all_to_all x0 -> x1, blocking collectives: none -> 17.5 us  [body(): both = lax.all_to_all(both, ('depth', 'row'), 0, 0, tiled=True)]
  transfers between devices with their start and end apart: 7 -> 43, of which waited for: 6 -> 21; matrix products, arithmetic and copies ran while one was open for 4% -> 11% of each run, Pallas kernels for 0% -> 0%
where the time goes in v1:
time: 690 us; the launch traced here: 688 us
  waiting for transfers between devices  466 us (68%)
  starting transfers between devices  81.6 us (12%)
  matrix products  59.7 us (9%)
  other arithmetic  36.3 us (5%)
  blocking collectives  17.5 us (3%)
  between operations  14.9 us (2%)
  local copies, waits for them, and re-layouts  12 us (2%)
    ppermute x9, waiting for transfers between devices, line_all_gather(): lax.ppermute(down, name, [(i, i - 1) for i in range(1, count - step + 1)])  186 us
    ppermute x9, waiting for transfers between devices, line_reduce_scatter(): up = lax.ppermute(send_up, name, [(i, i + 1) for i in range(step)])  139 us
    reduce_scatter x1, waiting for transfers between devices, body(): lax.psum_scatter(pre_near, 'depth', scatter_dimension=0, tiled=True)  84.1 us
    all_gather x1, waiting for transfers between devices, body(): far_pair = lax.all_gather(far_pair, 'depth', axis=0, tiled=False)  33.2 us
    ppermute x9, starting transfers between devices, line_reduce_scatter(): up = lax.ppermute(send_up, name, [(i, i + 1) for i in range(step)])  31.7 us
    dot_general x4, matrix products, product(): return jnp.dot(left, right, preferred_element_type=f32).astype(bf16)  29.5 us
    ppermute x9, starting transfers between devices, line_all_gather(): lax.ppermute(up, name, [(i, i + 1) for i in range(step - 1, count - 1)])  26.1 us
    all_to_all x1, blocking collectives, body(): both = lax.all_to_all(both, ('depth', 'row'), 0, 0, tiled=True)  17.5 us
  transfers between devices with their start and end apart: 43, of which 21 were waited for; matrix products, arithmetic and copies ran while one was open for 11% of the time, Pallas kernels for 0%

profile of v1, /device:TPU:0, one launch (start us, length us, event | category | flops | bytes accessed | tf_op | source)
XLA Modules:
  0.0 688.5 jit_solution(6808097987165497323)
XLA Ops:
  9.6 17.5 %all_to_all.10 = bf16[8,2,64,384]{3,2,1,0:T(8,128)(2,1)S(1)} all-to-all(bf16[8,2,64,384]{3,2,1,0:T(8,128)(2,1)S(1)} %bitcast.137), channel_id=1, replica_groups=mesh['depth'=4,'row'=2,'col'=4] {'depth','row'}, dimensions={0} | all-to-all | bytes 1572864 | tf_op jit(solution)/shard_map/all_to_all | solution.py:81
  27.2 10.5 %convolution_convert_fusion.1 = bf16[512,9216]{1,0:T(8,128)(2,1)} fusion(bf16[512,384]{1,0:T(8,128)(2,1)S(1)} %bitcast.129, bf16[384,12288]{1,0:T(8,128)(2,1)} %param.6), kind=kOutput, calls=%fused_computation.1 | convolution fusion | flops 3628597248 | bytes 16908288 | tf_op jit(solution)/shard_map/dot_general | solution.py:86
  37.8 10.5 %convolution_convert_fusion = bf16[512,9216]{1,0:T(8,128)(2,1)} fusion(bf16[512,384]{1,0:T(8,128)(2,1)S(1)} %bitcast.133, bf16[384,12288]{1,0:T(8,128)(2,1)} %param.7), kind=kOutput, calls=%fused_computation | convolution fusion | flops 3628597248 | bytes 16908288 | tf_op jit(solution)/shard_map/dot_general | solution.py:86
  48.2 84.1 %reduce-scatter.4.cloned.1.call-done = bf16[128,9216]{1,0:T(8,128)(2,1)} async-done(((bf16[512,9216]{1,0:T(8,128)(2,1)}), bf16[128,9216]{1,0:T(8,128)(2,1)}) %reduce-scatter.4.cloned.1.call-update) | async-done | bytes 2359312 | tf_op jit(solution)/shard_map/reduce_scatter | solution.py:94
  151.0 10.5 %collective-permute-done = bf16[32,9216]{1,0:T(8,128)(2,1)S(1)} collective-permute-done((bf16[32,9216]{1,0:T(8,128)(2,1)S(1)}, bf16[32,9216]{1,0:T(8,128)(2,1)S(1)}, u32[]{:S(2)}, u32[]{:S(2)}) %collective-permute-start) | collective-permute-done | bytes 589856 | tf_op jit(solution)/shard_map/ppermute | solution.py:36
  166.1 29.2 %collective-permute-done.24 = bf16[4,32,6144]{2,1,0:T(8,128)(2,1)S(1)} collective-permute-done((bf16[4,32,6144]{2,1,0:T(8,128)(2,1)S(1)}, bf16[4,32,6144]{2,1,0:T(8,128)(2,1)S(1)}, u32[]{:S(2)}, u32[]{:S(2)}) %collective-permute-start.24) | collective-permute-done | bytes 1572896 | tf_op jit(solution)/shard_map/ppermute | solution.py:36
  199.9 8.0 %collective-permute-done.1 = bf16[32,9216]{1,0:T(8,128)(2,1)S(1)} collective-permute-done((bf16[32,9216]{1,0:T(8,128)(2,1)S(1)}, bf16[32,9216]{1,0:T(8,128)(2,1)S(1)}, u32[]{:S(2)}, u32[]{:S(2)}) %collective-permute-start.1) | collective-permute-done | bytes 589856 | tf_op jit(solution)/shard_map/ppermute | solution.py:36
  208.8 31.2 %collective-permute-done.25 = bf16[4,32,6144]{2,1,0:T(8,128)(2,1)S(1)} collective-permute-done((bf16[4,32,6144]{2,1,0:T(8,128)(2,1)S(1)}, bf16[4,32,6144]{2,1,0:T(8,128)(2,1)S(1)}, u32[]{:S(2)}, u32[]{:S(2)}) %collective-permute-start.25) | collective-permute-done | bytes 1572896 | tf_op jit(solution)/shard_map/ppermute | solution.py:36
  253.3 37.6 %collective-permute-done.2 = bf16[32,9216]{1,0:T(8,128)(2,1)S(1)} collective-permute-done((bf16[32,9216]{1,0:T(8,128)(2,1)S(1)}, bf16[32,9216]{1,0:T(8,128)(2,1)S(1)}, u32[]{:S(2)}, u32[]{:S(2)}) %collective-permute-start.2) | collective-permute-done | bytes 589856 | tf_op jit(solution)/shard_map/ppermute | solution.py:36
  295.7 9.9 %collective-permute-start.6 = (bf16[32,9216]{1,0:T(8,128)(2,1)}, bf16[32,9216]{1,0:T(8,128)(2,1)}, u32[]{:S(2)}, u32[]{:S(2)}) collective-permute-start(bf16[32,9216]{1,0:T(8,128)(2,1)} %get-tuple-element.14), channel_id=1, source_target_pairs={{0,1},{1,2},{2,3},{4,5},{5,6},{6,7},{8,9},{9,10},{10,11},{12,13},{... | collective-permute-start | bytes 1769480 | tf_op jit(solution)/shard_map/ppermute | solution.py:50
  305.6 25.3 %collective-permute-done.7 = bf16[32,9216]{1,0:T(8,128)(2,1)} collective-permute-done((bf16[32,9216]{1,0:T(8,128)(2,1)}, bf16[32,9216]{1,0:T(8,128)(2,1)}, u32[]{:S(2)}, u32[]{:S(2)}) %collective-permute-start.7) | collective-permute-done | bytes 589856 | tf_op jit(solution)/shard_map/ppermute | solution.py:51
  333.8 21.1 %collective-permute-done.8 = bf16[32,9216]{1,0:T(8,128)(2,1)} collective-permute-done((bf16[32,9216]{1,0:T(8,128)(2,1)}, bf16[32,9216]{1,0:T(8,128)(2,1)}, u32[]{:S(2)}, u32[]{:S(2)}) %collective-permute-start.8) | collective-permute-done | bytes 589856 | tf_op jit(solution)/shard_map/ppermute | solution.py:51
  361.2 8.0 %collective-permute-done.9 = bf16[32,9216]{1,0:T(8,128)(2,1)} collective-permute-done((bf16[32,9216]{1,0:T(8,128)(2,1)}, bf16[32,9216]{1,0:T(8,128)(2,1)}, u32[]{:S(2)}, u32[]{:S(2)}) %collective-permute-start.9) | collective-permute-done | bytes 589856 | tf_op jit(solution)/shard_map/ppermute | solution.py:51
  379.3 8.3 %collective-permute-done.12 = bf16[32,9216]{1,0:T(8,128)(2,1)S(1)} collective-permute-done((bf16[32,9216]{1,0:T(8,128)(2,1)S(1)}, bf16[32,9216]{1,0:T(8,128)(2,1)S(1)}, u32[]{:S(2)}, u32[]{:S(2)}) %collective-permute-start.12) | collective-permute-done | bytes 589856 | tf_op jit(solution)/shard_map/ppermute | solution.py:36
  413.4 13.3 %collective-permute-done.17 = bf16[32,9216]{1,0:T(8,128)(2,1)S(1)} collective-permute-done((bf16[32,9216]{1,0:T(8,128)(2,1)S(1)}, bf16[32,9216]{1,0:T(8,128)(2,1)S(1)}, u32[]{:S(2)}, u32[]{:S(2)}) %collective-permute-start.17) | collective-permute-done | bytes 589856 | tf_op jit(solution)/shard_map/ppermute | solution.py:37
  449.2 14.0 %collective-permute-done.20 = bf16[32,9216]{1,0:T(8,128)(2,1)} collective-permute-done((bf16[32,9216]{1,0:T(8,128)(2,1)}, bf16[32,9216]{1,0:T(8,128)(2,1)}, u32[]{:S(2)}, u32[]{:S(2)}) %collective-permute-start.20) | collective-permute-done | bytes 589856 | tf_op jit(solution)/shard_map/ppermute | solution.py:51
  466.0 9.2 %collective-permute-done.21 = bf16[32,9216]{1,0:T(8,128)(2,1)} collective-permute-done((bf16[32,9216]{1,0:T(8,128)(2,1)}, bf16[32,9216]{1,0:T(8,128)(2,1)}, u32[]{:S(2)}, u32[]{:S(2)}) %collective-permute-start.21) | collective-permute-done | bytes 589856 | tf_op jit(solution)/shard_map/ppermute | solution.py:51
  479.0 11.4 %all-gather.5.cloned.1.call-done = bf16[512,9216]{1,0:T(8,128)(2,1)} async-done(((bf16[128,9216]{1,0:T(8,128)(2,1)}), bf16[512,9216]{1,0:T(8,128)(2,1)}) %all-gather.5.cloned.1.call-update) | async-done | bytes 9437200 | tf_op jit(solution)/shard_map/all_gather | solution.py:120
  490.4 33.2 %all-gather.9.cloned.1.call-done = bf16[128,6144]{1,0:T(8,128)(2,1)} async-done(((bf16[32,6144]{1,0:T(8,128)(2,1)}), bf16[128,6144]{1,0:T(8,128)(2,1)}) %all-gather.9.cloned.1.call-update) | async-done | bytes 1572880 | tf_op jit(solution)/shard_map/all_gather | solution.py:118
  529.6 32.3 %collective-permute-done.31 = bf16[4,32,6144]{2,1,0:T(8,128)(2,1)S(1)} collective-permute-done((bf16[4,32,6144]{2,1,0:T(8,128)(2,1)}, bf16[4,32,6144]{2,1,0:T(8,128)(2,1)S(1)}, u32[]{:S(2)}, u32[]{:S(2)}) %collective-permute-start.31) | collective-permute-done | bytes 1572896 | tf_op jit(solution)/shard_map/ppermute | solution.py:51
  563.9 35.2 %collective-permute-done.32 = bf16[4,32,6144]{2,1,0:T(8,128)(2,1)S(1)} collective-permute-done((bf16[4,32,6144]{2,1,0:T(8,128)(2,1)S(1)}, bf16[4,32,6144]{2,1,0:T(8,128)(2,1)S(1)}, u32[]{:S(2)}, u32[]{:S(2)}) %collective-permute-start.32) | collective-permute-done | bytes 1572896 | tf_op jit(solution)/shard_map/ppermute | solution.py:51
  603.0 32.5 %collective-permute-done.33 = bf16[4,32,6144]{2,1,0:T(8,128)(2,1)S(1)} collective-permute-done((bf16[4,32,6144]{2,1,0:T(8,128)(2,1)S(1)}, bf16[4,32,6144]{2,1,0:T(8,128)(2,1)S(1)}, u32[]{:S(2)}, u32[]{:S(2)}) %collective-permute-start.33) | collective-permute-done | bytes 1572896 | tf_op jit(solution)/shard_map/ppermute | solution.py:51
  650.5 9.7 %fusion.1 = f32[512,384]{1,0:T(8,128)S(1)} fusion(bf16[512,9216]{1,0:T(8,128)(2,1)} %all-gather.7.cloned.1.call-done, bf16[384,12288]{1,0:T(8,128)(2,1)} %param.6), kind=kOutput, calls=%fused_computation.8 | convolution fusion | flops 3623878656 | bytes 17301504 | tf_op jit(solution)/shard_map/dot_general | solution.py:134
  668.9 8.1 %convolution_convert_fusion.3 = bf16[384,9216]{1,0:T(8,128)(2,1)S(1)} fusion(bf16[512,384]{1,0:T(8,128)(2,1)S(1)} %bitcast.132, bf16[512,9216]{1,0:T(8,128)(2,1)} %all-gather.7.cloned.1.call-done), kind=kOutput, calls=%fused_computation.3 | convolution fusion | flops 3627417600 | bytes 16908288 | tf_op jit(solution)/shard_map/dot_general | solution.py:89
  (152 shorter events, 163.0 us)
Async XLA Ops:
  7.2 125.1 %reduce-scatter.4.cloned.1.call-start = ((), (), s32[]{:S(2)}) async-start(), calls=%async_computation.5 | async-start | bytes 11796480 | tf_op jit(solution)/shard_map/reduce_scatter | solution.py:94
  37.7 337.7 %reduce-scatter.6.cloned.1.call-start = ((), (), s32[]{:S(2)}) async-start(), calls=%async_computation.7 | async-start | bytes 11796480 | tf_op jit(solution)/shard_map/reduce_scatter | solution.py:103
  132.3 299.4 %reduce-scatter.8.cloned.1.call-start = ((), (), s32[]{:S(2)}) async-start(), calls=%async_computation.9 | async-start | bytes 1966080 | tf_op jit(solution)/shard_map/reduce_scatter | solution.py:105
  148.2 47.1 %collective-permute-start.24 = (bf16[4,32,6144]{2,1,0:T(8,128)(2,1)S(1)}, bf16[4,32,6144]{2,1,0:T(8,128)(2,1)S(1)}, u32[]{:S(2)}, u32[]{:S(2)}) collective-permute-start(bf16[4,32,6144]{2,1,0:T(8,128)(2,1)S(1)} %get-tuple-element.17), channel_id=1, source_target_pairs={{0,1},{4,5},{8,9},{12,13},{16,17},{20,21},{24,25},{28,29}} | collective-permute-start | bytes 4718600 | tf_op jit(solution)/shard_map/ppermute | solution.py:36
  149.5 59.2 %collective-permute-start.27 = (bf16[4,32,6144]{2,1,0:T(8,128)(2,1)S(1)}, bf16[4,32,6144]{2,1,0:T(8,128)(2,1)S(1)}, u32[]{:S(2)}, u32[]{:S(2)}) collective-permute-start(bf16[4,32,6144]{2,1,0:T(8,128)(2,1)S(1)} %get-tuple-element.18), channel_id=1, source_target_pairs={{3,2},{7,6},{11,10},{15,14},{19,18},{23,22},{27,26},{31,30}} | collective-permute-start | bytes 4718600 | tf_op jit(solution)/shard_map/ppermute | solution.py:37
  150.3 49.6 %collective-permute-start.3 = (bf16[32,9216]{1,0:T(8,128)(2,1)S(1)}, bf16[32,9216]{1,0:T(8,128)(2,1)S(1)}, u32[]{:S(2)}, u32[]{:S(2)}) collective-permute-start(bf16[32,9216]{1,0:T(8,128)(2,1)S(1)} %get-tuple-element.26), channel_id=1, source_target_pairs={{3,2},{7,6},{11,10},{15,14},{19,18},{23,22},{27,26},{31,30}} | collective-permute-start | bytes 1769480 | tf_op jit(solution)/shard_map/ppermute | solution.py:37
  161.6 46.3 %collective-permute-start.1 = (bf16[32,9216]{1,0:T(8,128)(2,1)S(1)}, bf16[32,9216]{1,0:T(8,128)(2,1)S(1)}, u32[]{:S(2)}, u32[]{:S(2)}) collective-permute-start(bf16[32,9216]{1,0:T(8,128)(2,1)S(1)} %bitcast_add_fusion.10), channel_id=1, source_target_pairs={{0,1},{1,2},{4,5},{5,6},{8,9},{9,10},{12,13},{13,14},{16,17},{17,1... | collective-permute-start | bytes 1769480 | tf_op jit(solution)/shard_map/ppermute | solution.py:36
  195.4 44.6 %collective-permute-start.25 = (bf16[4,32,6144]{2,1,0:T(8,128)(2,1)S(1)}, bf16[4,32,6144]{2,1,0:T(8,128)(2,1)S(1)}, u32[]{:S(2)}, u32[]{:S(2)}) collective-permute-start(bf16[4,32,6144]{2,1,0:T(8,128)(2,1)S(1)} %bitcast_add_fusion.2), channel_id=1, source_target_pairs={{0,1},{1,2},{4,5},{5,6},{8,9},{9,10},{12,13},{13,14},{16,17},{17,1... | collective-permute-start | bytes 4718600 | tf_op jit(solution)/shard_map/ppermute | solution.py:36
  208.0 41.1 %collective-permute-start.4 = (bf16[32,9216]{1,0:T(8,128)(2,1)S(1)}, bf16[32,9216]{1,0:T(8,128)(2,1)S(1)}, u32[]{:S(2)}, u32[]{:S(2)}) collective-permute-start(bf16[32,9216]{1,0:T(8,128)(2,1)S(1)} %get-tuple-element.24), channel_id=1, source_target_pairs={{2,1},{3,2},{6,5},{7,6},{10,9},{11,10},{14,13},{15,14},{18,17},{19... | collective-permute-start | bytes 1769480 | tf_op jit(solution)/shard_map/ppermute | solution.py:37
  241.5 114.7 %collective-permute-start.26 = (bf16[4,32,6144]{2,1,0:T(8,128)(2,1)}, bf16[4,32,6144]{2,1,0:T(8,128)(2,1)}, u32[]{:S(2)}, u32[]{:S(2)}) collective-permute-start(bf16[4,32,6144]{2,1,0:T(8,128)(2,1)} %get-tuple-element.15), channel_id=1, source_target_pairs={{0,1},{1,2},{2,3},{4,5},{5,6},{6,7},{8,9},{9,10},{10,11},{12,13},{... | collective-permute-start | bytes 4718600 | tf_op jit(solution)/shard_map/ppermute | solution.py:36
  247.8 43.2 %collective-permute-start.2 = (bf16[32,9216]{1,0:T(8,128)(2,1)S(1)}, bf16[32,9216]{1,0:T(8,128)(2,1)S(1)}, u32[]{:S(2)}, u32[]{:S(2)}) collective-permute-start(bf16[32,9216]{1,0:T(8,128)(2,1)S(1)} %get-tuple-element.23), channel_id=1, source_target_pairs={{0,1},{1,2},{2,3},{4,5},{5,6},{6,7},{8,9},{9,10},{10,11},{12,13},{... | collective-permute-start | bytes 1769480 | tf_op jit(solution)/shard_map/ppermute | solution.py:36
  249.2 41.8 %collective-permute-start.5 = (bf16[32,9216]{1,0:T(8,128)(2,1)S(1)}, bf16[32,9216]{1,0:T(8,128)(2,1)S(1)}, u32[]{:S(2)}, u32[]{:S(2)}) collective-permute-start(bf16[32,9216]{1,0:T(8,128)(2,1)S(1)} %bitcast_add_fusion.9), channel_id=1, source_target_pairs={{1,0},{2,1},{3,2},{5,4},{6,5},{7,6},{9,8},{10,9},{11,10},{13,12},{... | collective-permute-start | bytes 1769480 | tf_op jit(solution)/shard_map/ppermute | solution.py:37
  251.9 104.3 %collective-permute-start.29 = (bf16[4,32,6144]{2,1,0:T(8,128)(2,1)}, bf16[4,32,6144]{2,1,0:T(8,128)(2,1)}, u32[]{:S(2)}, u32[]{:S(2)}) collective-permute-start(bf16[4,32,6144]{2,1,0:T(8,128)(2,1)} %bitcast_add_fusion.1), channel_id=1, source_target_pairs={{1,0},{2,1},{3,2},{5,4},{6,5},{7,6},{9,8},{10,9},{11,10},{13,12},{... | collective-permute-start | bytes 4718600 | tf_op jit(solution)/shard_map/ppermute | solution.py:37
  294.4 36.5 %collective-permute-start.7 = (bf16[32,9216]{1,0:T(8,128)(2,1)}, bf16[32,9216]{1,0:T(8,128)(2,1)}, u32[]{:S(2)}, u32[]{:S(2)}) collective-permute-start(bf16[32,9216]{1,0:T(8,128)(2,1)} %get-tuple-element.14), channel_id=1, source_target_pairs={{1,0},{2,1},{3,2},{5,4},{6,5},{7,6},{9,8},{10,9},{11,10},{13,12},{... | collective-permute-start | bytes 1769480 | tf_op jit(solution)/shard_map/ppermute | solution.py:51
  295.7 36.6 %collective-permute-start.6 = (bf16[32,9216]{1,0:T(8,128)(2,1)}, bf16[32,9216]{1,0:T(8,128)(2,1)}, u32[]{:S(2)}, u32[]{:S(2)}) collective-permute-start(bf16[32,9216]{1,0:T(8,128)(2,1)} %get-tuple-element.14), channel_id=1, source_target_pairs={{0,1},{1,2},{2,3},{4,5},{5,6},{6,7},{8,9},{9,10},{10,11},{12,13},{... | collective-permute-start | bytes 1769480 | tf_op jit(solution)/shard_map/ppermute | solution.py:50
  360.4 129.9 %all-gather.5.cloned.1.call-start = ((), (), s32[]{:S(2)}) async-start(), calls=%async_computation.6 | async-start | bytes 11796480 | tf_op jit(solution)/shard_map/all_gather | solution.py:120
  375.3 148.3 %all-gather.9.cloned.1.call-start = ((), (), s32[]{:S(2)}) async-start(), calls=%async_computation.10 | async-start | bytes 1966080 | tf_op jit(solution)/shard_map/all_gather | solution.py:118
  465.3 185.2 %all-gather.7.cloned.1.call-start = ((), (), s32[]{:S(2)}) async-start(), calls=%async_computation.8 | async-start | bytes 11796480 | tf_op jit(solution)/shard_map/all_gather | solution.py:123
  523.6 38.2 %collective-permute-start.31 = (bf16[4,32,6144]{2,1,0:T(8,128)(2,1)}, bf16[4,32,6144]{2,1,0:T(8,128)(2,1)S(1)}, u32[]{:S(2)}, u32[]{:S(2)}) collective-permute-start(bf16[4,32,6144]{2,1,0:T(8,128)(2,1)} %bitcast.138), channel_id=1, source_target_pairs={{1,0},{2,1},{3,2},{5,4},{6,5},{7,6},{9,8},{10,9},{11,10},{13,12},{... | collective-permute-start | bytes 4718600 | tf_op jit(solution)/shard_map/ppermute | solution.py:51
  524.9 38.2 %collective-permute-start.30 = (bf16[4,32,6144]{2,1,0:T(8,128)(2,1)}, bf16[4,32,6144]{2,1,0:T(8,128)(2,1)S(1)}, u32[]{:S(2)}, u32[]{:S(2)}) collective-permute-start(bf16[4,32,6144]{2,1,0:T(8,128)(2,1)} %bitcast.139), channel_id=1, source_target_pairs={{0,1},{1,2},{2,3},{4,5},{5,6},{6,7},{8,9},{9,10},{10,11},{12,13},{... | collective-permute-start | bytes 4718600 | tf_op jit(solution)/shard_map/ppermute | solution.py:50
  561.8 37.2 %collective-permute-start.32 = (bf16[4,32,6144]{2,1,0:T(8,128)(2,1)S(1)}, bf16[4,32,6144]{2,1,0:T(8,128)(2,1)S(1)}, u32[]{:S(2)}, u32[]{:S(2)}) collective-permute-start(bf16[4,32,6144]{2,1,0:T(8,128)(2,1)S(1)} %collective-permute-done.31), channel_id=1, source_target_pairs={{1,0},{2,1},{5,4},{6,5},{9,8},{10,9},{13,12},{14,13},{17,16},{18,1... | collective-permute-start | bytes 4718600 | tf_op jit(solution)/shard_map/ppermute | solution.py:51
  563.1 38.8 %collective-permute-start.34 = (bf16[4,32,6144]{2,1,0:T(8,128)(2,1)S(1)}, bf16[4,32,6144]{2,1,0:T(8,128)(2,1)S(1)}, u32[]{:S(2)}, u32[]{:S(2)}) collective-permute-start(bf16[4,32,6144]{2,1,0:T(8,128)(2,1)S(1)} %collective-permute-done.30), channel_id=1, source_target_pairs={{1,2},{2,3},{5,6},{6,7},{9,10},{10,11},{13,14},{14,15},{17,18},{18... | collective-permute-start | bytes 4718600 | tf_op jit(solution)/shard_map/ppermute | solution.py:50
  599.1 36.4 %collective-permute-start.33 = (bf16[4,32,6144]{2,1,0:T(8,128)(2,1)S(1)}, bf16[4,32,6144]{2,1,0:T(8,128)(2,1)S(1)}, u32[]{:S(2)}, u32[]{:S(2)}) collective-permute-start(bf16[4,32,6144]{2,1,0:T(8,128)(2,1)S(1)} %collective-permute-done.32), channel_id=1, source_target_pairs={{1,0},{5,4},{9,8},{13,12},{17,16},{21,20},{25,24},{29,28}} | collective-permute-start | bytes 4718600 | tf_op jit(solution)/shard_map/ppermute | solution.py:51
  602.0 34.7 %collective-permute-start.35 = (bf16[4,32,6144]{2,1,0:T(8,128)(2,1)S(1)}, bf16[4,32,6144]{2,1,0:T(8,128)(2,1)S(1)}, u32[]{:S(2)}, u32[]{:S(2)}) collective-permute-start(bf16[4,32,6144]{2,1,0:T(8,128)(2,1)S(1)} %collective-permute-done.34), channel_id=1, source_target_pairs={{2,3},{6,7},{10,11},{14,15},{18,19},{22,23},{26,27},{30,31}} | collective-permute-start | bytes 4718600 | tf_op jit(solution)/shard_map/ppermute | solution.py:50
  (34 other events, 541.2 us)
Sparse Core Ops, SparseCore 0:
  37.8 94.4 reduce-scatter.3
  136.0 95.0 reduce-scatter.5
  360.6 31.6 reduce-scatter.7
  394.0 96.3 all-gather.4
  492.6 30.9 all-gather.8
  525.3 96.3 all-gather.6

commit v2 on v1

v2 whole, which is shorter than its diff:
```python
import math

import jax
import jax.numpy as jnp
from jax import lax
from jax.sharding import PartitionSpec as P


def gelu_parts(hidden):
    coeff = math.sqrt(2.0 / math.pi)
    cube = hidden * hidden * hidden
    slope_in = jnp.tanh(coeff * (hidden + 0.044715 * cube))
    value = 0.5 * hidden * (1.0 + slope_in)
    slope = 0.5 * (1.0 + slope_in) + 0.5 * hidden * (1.0 - slope_in * slope_in) * coeff * (
        1.0 + 3.0 * 0.044715 * hidden * hidden
    )
    return (value, slope)


def line_sums(parts, axis, name, steps, carry=None):
    count = lax.axis_size(name)
    here = lax.axis_index(name)

    def piece(index):
        return lax.dynamic_index_in_dim(
            parts, jnp.clip(index, 0, count - 1), axis, keepdims=False
        )

    for step in steps:
        send_up = piece(here + count - step)
        send_down = piece(here + step - count)
        if carry is not None:
            send_up, send_down = send_up + carry[0], send_down + carry[1]
        carry = (
            lax.ppermute(send_up, name, [(i, i + 1) for i in range(step)]),
            lax.ppermute(send_down, name, [(i, i - 1) for i in range(count - step, count)]),
        )
    return carry


def line_total(parts, axis, name, carry):
    own = lax.dynamic_index_in_dim(parts, lax.axis_index(name), axis, keepdims=False)
    up, down = carry
    return own.astype(jnp.float32) + up.astype(jnp.float32) + down.astype(jnp.float32)


def line_moves(block, name, steps, carry=None):
    count = lax.axis_size(name)
    ups, downs = carry if carry is not None else ([], [])
    for step in steps:
        up = ups[-1] if ups else block
        down = downs[-1] if downs else block
        ups = ups + [lax.ppermute(up, name, [(i, i + 1) for i in range(step - 1, count - 1)])]
        downs = downs + [lax.ppermute(down, name, [(i, i - 1) for i in range(1, count - step + 1)])]
    return ups, downs


def line_whole(block, axis, name, carry):
    count = lax.axis_size(name)
    here = lax.axis_index(name)
    ups, downs = carry
    shape = block.shape[:axis] + (count,) + block.shape[axis:]
    whole = lax.dynamic_update_index_in_dim(
        jnp.zeros(shape, block.dtype), block, here, axis
    )
    for step in range(1, count):
        arrived = jnp.where(here >= step, ups[step - 1], downs[count - step - 1])
        whole = lax.dynamic_update_index_in_dim(
            whole, arrived, lax.rem(here - step + count, count), axis
        )
    return whole


def body(tokens, grad_out, w_up, w_down):
    n_depth, n_row, n_col = (lax.axis_size(a) for a in ("depth", "row", "col"))
    rows, part = tokens.shape
    narrow, hidden = w_up.shape
    group = n_depth * n_row
    total = group * rows
    bunch = total // (n_depth * n_col)
    far = hidden // 4 // 128 * 128
    near = hidden - far
    bf16, f32 = jnp.bfloat16, jnp.float32

    both = jnp.stack([tokens, grad_out]).reshape(2, rows, n_depth, narrow)
    both = jnp.transpose(both, (2, 0, 1, 3))
    both = jnp.broadcast_to(both[:, None], (n_depth, n_row, 2, rows, narrow))
    both = both.reshape(group, 2, rows, narrow)
    both = lax.all_to_all(both, ("depth", "row"), 0, 0, tiled=True)
    x_cols = both[:, 0].reshape(total, narrow)
    dy_cols = both[:, 1].reshape(total, narrow)

    def product(left, right):
        return jnp.dot(left, right, preferred_element_type=f32).astype(bf16)

    def outer(left, right):
        return lax.dot_general(
            left, right, (((0,), (0,)), ((), ())), preferred_element_type=f32
        ).astype(bf16)

    steps = range(1, n_col)
    third = max(1, (n_col - 1) // 3)
    tie = lax.optimization_barrier

    pre_near = product(x_cols, w_up[:, :near])
    pre_near = lax.psum_scatter(pre_near, "depth", scatter_dimension=0, tiled=True)
    far_terms = jnp.concatenate(
        [product(x_cols, w_up[:, near:]), product(dy_cols, w_down[:, near:])], axis=1
    ).reshape(n_depth, n_col, bunch, 2 * far)
    far_move = line_sums(far_terms, 1, "col", steps[:-third])
    grad_near = product(dy_cols, w_down[:, :near])
    pre_near, grad_near, far_move = tie((pre_near, grad_near, far_move))

    grad_near = lax.psum_scatter(grad_near, "depth", scatter_dimension=0, tiled=True)
    far_move = line_sums(far_terms, 1, "col", steps[-third:], far_move)
    far_sum = line_total(far_terms, 1, "col", far_move).astype(bf16)
    pre_near = pre_near.reshape(n_col, bunch, near)
    pre_move = line_sums(pre_near, 0, "col", steps)
    grad_near, far_sum, pre_move = tie((grad_near, far_sum, pre_move))

    far_sum = lax.psum_scatter(
        far_sum.reshape(n_depth * bunch, 2 * far), "depth", scatter_dimension=0, tiled=True
    )
    grad_near = grad_near.reshape(n_col, bunch, near)
    grad_move = line_sums(grad_near, 0, "col", steps[:-third])
    far_sum, grad_move = tie((far_sum, grad_move))

    far_sum = far_sum.astype(f32)
    far_value, far_slope = gelu_parts(far_sum[:, :far])
    far_pair = jnp.concatenate(
        [far_value.astype(bf16), (far_sum[:, far:] * far_slope).astype(bf16)], axis=1
    )
    far_pair = lax.all_gather(far_pair, "depth", axis=0, tiled=False)
    grad_move = line_sums(grad_near, 0, "col", steps[-third:], grad_move)
    near_value, near_slope = gelu_parts(line_total(pre_near, 0, "col", pre_move))
    act_near = near_value.astype(bf16)
    hid_near = (line_total(grad_near, 0, "col", grad_move) * near_slope).astype(bf16)
    hid_move = line_moves(hid_near, "col", steps)
    far_pair, hid_near, hid_move = tie((far_pair, hid_near, hid_move))

    hid_near = line_whole(hid_near, 0, "col", hid_move).reshape(n_col * bunch, near)
    hid_near = lax.all_gather(hid_near, "depth", axis=0, tiled=True)
    act_move = line_moves(act_near, "col", steps)
    act_near = line_whole(act_near, 0, "col", act_move).reshape(n_col * bunch, near)
    far_move = line_moves(far_pair, "col", steps[:third])
    hid_near, act_near, far_move = tie((hid_near, act_near, far_move))

    act_near = lax.all_gather(act_near, "depth", axis=0, tiled=True)
    far_move = line_moves(far_pair, "col", steps[third:], far_move)
    far_pair = line_whole(far_pair, 1, "col", far_move).reshape(total, 2 * far)
    act_far, hid_far = far_pair[:, :far], far_pair[:, far:]

    def back(left, right):
        return lax.dot_general(
            left, right, (((1,), (1,)), ((), ())), preferred_element_type=f32
        )

    grad_in = back(hid_near, w_up[:, :near]) + back(hid_far, w_up[:, near:])
    grad_in = grad_in.astype(bf16).reshape(group, rows, narrow)
    grad_in = lax.all_to_all(grad_in, ("depth", "row"), 0, 0, tiled=True)
    grad_in = grad_in.reshape(n_depth, n_row, rows, narrow).astype(f32).sum(axis=1)
    grad_in = jnp.transpose(grad_in, (1, 0, 2)).reshape(rows, part).astype(bf16)
    grad_up = jnp.concatenate([outer(x_cols, hid_near), outer(x_cols, hid_far)], axis=1)
    down_far = outer(dy_cols, act_far)
    act_near, grad_in, grad_up, down_far = tie((act_near, grad_in, grad_up, down_far))
    grad_down = jnp.concatenate([outer(dy_cols, act_near), down_far], axis=1)
    return (grad_in, grad_up, grad_down)


def solution(mesh):
    placed = (
        P(("depth", "row"), "col"),
        P(("depth", "row"), "col"),
        P(("col", "depth"), "row"),
        P(("col", "depth"), "row"),
    )
    return jax.shard_map(
        body,
        mesh=mesh,
        in_specs=placed,
        out_specs=(
            P(("depth", "row"), "col"),
            P(("col", "depth"), "row"),
            P(("col", "depth"), "row"),
        ),
        check_vma=False,
    )
```

time: 690 us -> 574 us (0.83)
  waiting for transfers between devices: 466 us -> 298 us
  starting transfers between devices: 81.6 us -> 104 us
  other arithmetic: 36.3 us -> 49 us
  local copies, waits for them, and re-layouts: 12 us -> 20.3 us
    reduce_scatter x1, waiting for transfers between devices: 84.1 us -> 0.69 us  [body(): lax.psum_scatter(pre_near, 'depth', scatter_dimension=0, tiled=True)]
    ppermute x36, waiting for transfers between devices: 338 us -> 276 us  [the longest x9 121 us: line_sums(): lax.ppermute(send_up, name, [(i, i + 1) for i in range(step)])]
    all_gather x1, waiting for transfers between devices: 33.2 us -> 0.01 us  [body(): far_pair = lax.all_gather(far_pair, 'depth', axis=0, tiled=False)]
    ppermute x36, starting transfers between devices: 78 us -> 100 us  [the longest x9 60.7 us: line_sums(): lax.ppermute(send_up, name, [(i, i + 1) for i in range(step)])]
    all_gather x1, waiting for transfers between devices: 0.01 us -> 15.3 us  [body(): hid_near = lax.all_gather(hid_near, 'depth', axis=0, tiled=True)]
    all_gather x1, waiting for transfers between devices: 11.4 us -> 0.73 us  [body(): act_near = lax.all_gather(act_near, 'depth', axis=0, tiled=True)]
    add x9 -> x7, other arithmetic: 3.62 us -> 14.2 us  [line_sums(): send_up, send_down = (send_up + carry[0], send_down + carry[1])]
    dynamic_update_slice x11 -> x10, other arithmetic: 15 us -> 13.6 us  [the longest x9 10.9 us: line_whole(): lax.dynamic_update_index_in_dim(whole, arrived, lax.rem(here - step + cou...]
  transfers between devices with their start and end apart: 43 -> 43, of which waited for: 21 -> 28; matrix products, arithmetic and copies ran while one was open for 11% -> 16% of each run, Pallas kernels for 0% -> 0%
where the time goes in v2:
time: 574 us; the launch traced here: 566 us
  waiting for transfers between devices  298 us (52%)
  starting transfers between devices  104 us (18%)
  matrix products  62.8 us (11%)
  other arithmetic  49 us (9%)
  local copies, waits for them, and re-layouts  20.3 us (4%)
  blocking collectives  17.5 us (3%)
  between operations  14.7 us (3%)
    ppermute x9, waiting for transfers between devices, line_sums(): lax.ppermute(send_up, name, [(i, i + 1) for i in range(step)])  121 us
    ppermute x9, waiting for transfers between devices, line_moves(): lax.ppermute(down, name, [(i, i - 1) for i in range(1, count - step + 1)])  116 us
    ppermute x9, starting transfers between devices, line_sums(): lax.ppermute(send_up, name, [(i, i + 1) for i in range(step)])  60.7 us
    ppermute x9, waiting for transfers between devices, line_moves(): lax.ppermute(up, name, [(i, i + 1) for i in range(step - 1, count - 1)])  31.6 us
    dot_general x4, matrix products, product(): return jnp.dot(left, right, preferred_element_type=f32).astype(bf16)  29.5 us
    dot_general x4, matrix products, outer(): lax.dot_general(left, right, (((0,), (0,)), ((), ())), preferred_element_...  19 us
    all_to_all x1, blocking collectives, body(): both = lax.all_to_all(both, ('depth', 'row'), 0, 0, tiled=True)  17.5 us
    all_gather x1, waiting for transfers between devices, body(): hid_near = lax.all_gather(hid_near, 'depth', axis=0, tiled=True)  15.3 us
  transfers between devices with their start and end apart: 43, of which 28 were waited for; matrix products, arithmetic and copies ran while one was open for 16% of the time, Pallas kernels for 0%

profile of v2, /device:TPU:0, one launch (start us, length us, event | category | flops | bytes accessed | tf_op | source)
XLA Modules:
  0.0 566.0 jit_solution(11642848710837175155)
XLA Ops:
  9.6 17.5 %all_to_all.10 = bf16[8,2,64,384]{3,2,1,0:T(8,128)(2,1)S(1)} all-to-all(bf16[8,2,64,384]{3,2,1,0:T(8,128)(2,1)S(1)} %bitcast.135), channel_id=1, replica_groups=mesh['depth'=4,'row'=2,'col'=4] {'depth','row'}, dimensions={0} | all-to-all | bytes 1572864 | tf_op jit(solution)/shard_map/all_to_all | solution.py:89
  27.2 10.5 %convolution_convert_fusion.1 = bf16[512,9216]{1,0:T(8,128)(2,1)} fusion(bf16[512,384]{1,0:T(8,128)(2,1)S(1)} %bitcast.131, bf16[384,12288]{1,0:T(8,128)(2,1)} %param.6), kind=kOutput, calls=%fused_computation.1 | convolution fusion | flops 3628597248 | bytes 16908288 | tf_op jit(solution)/shard_map/dot_general | solution.py:94
  58.1 31.3 %collective-permute-done = bf16[4,32,6144]{2,1,0:T(8,128)(2,1)S(1)} collective-permute-done((bf16[4,32,6144]{2,1,0:T(8,128)(2,1)}, bf16[4,32,6144]{2,1,0:T(8,128)(2,1)S(1)}, u32[]{:S(2)}, u32[]{:S(2)}) %collective-permute-start) | collective-permute-done | bytes 1572896 | tf_op jit(solution)/shard_map/ppermute | solution.py:35
  100.1 10.4 %convolution_convert_fusion = bf16[512,9216]{1,0:T(8,128)(2,1)} fusion(bf16[512,384]{1,0:T(8,128)(2,1)S(1)} %bitcast.128, bf16[384,12288]{1,0:T(8,128)(2,1)} %param.7), kind=kOutput, calls=%fused_computation | convolution fusion | flops 3628597248 | bytes 16908288 | tf_op jit(solution)/shard_map/dot_general | solution.py:94
  110.5 19.9 %collective-permute-done.1 = bf16[4,32,6144]{2,1,0:T(8,128)(2,1)S(1)} collective-permute-done((bf16[4,32,6144]{2,1,0:T(8,128)(2,1)}, bf16[4,32,6144]{2,1,0:T(8,128)(2,1)S(1)}, u32[]{:S(2)}, u32[]{:S(2)}) %collective-permute-start.1) | collective-permute-done | bytes 1572896 | tf_op jit(solution)/shard_map/ppermute | solution.py:35
  135.6 7.4 %collective-permute-start.6 = (bf16[32,9216]{1,0:T(8,128)(2,1)}, bf16[32,9216]{1,0:T(8,128)(2,1)}, u32[]{:S(2)}, u32[]{:S(2)}) collective-permute-start(bf16[32,9216]{1,0:T(8,128)(2,1)} %get-tuple-element.74), channel_id=1, source_target_pairs={{0,1},{4,5},{8,9},{12,13},{16,17},{20,21},{24,25},{28,29}} | collective-permute-start | bytes 1769480 | tf_op jit(solution)/shard_map/ppermute | solution.py:35
  153.8 18.5 %collective-permute-start.7 = (bf16[32,9216]{1,0:T(8,128)(2,1)S(1)}, bf16[32,9216]{1,0:T(8,128)(2,1)S(1)}, u32[]{:S(2)}, u32[]{:S(2)}) collective-permute-start(bf16[32,9216]{1,0:T(8,128)(2,1)S(1)} %get-tuple-element.72), channel_id=1, source_target_pairs={{0,1},{1,2},{4,5},{5,6},{8,9},{9,10},{12,13},{13,14},{16,17},{17,1... | collective-permute-start | bytes 1769480 | tf_op jit(solution)/shard_map/ppermute | solution.py:35
  191.3 28.4 %collective-permute-done.4 = bf16[4,32,6144]{2,1,0:T(8,128)(2,1)S(1)} collective-permute-done((bf16[4,32,6144]{2,1,0:T(8,128)(2,1)S(1)}, bf16[4,32,6144]{2,1,0:T(8,128)(2,1)S(1)}, u32[]{:S(2)}, u32[]{:S(2)}) %collective-permute-start.4) | collective-permute-done | bytes 1572896 | tf_op jit(solution)/shard_map/ppermute | solution.py:35
  239.2 10.4 %collective-permute-done.12 = bf16[32,9216]{1,0:T(8,128)(2,1)} collective-permute-done((bf16[32,9216]{1,0:T(8,128)(2,1)}, bf16[32,9216]{1,0:T(8,128)(2,1)}, u32[]{:S(2)}, u32[]{:S(2)}) %collective-permute-start.12) | collective-permute-done | bytes 589856 | tf_op jit(solution)/shard_map/ppermute | solution.py:35
  258.1 9.3 %collective-permute-done.13 = bf16[32,9216]{1,0:T(8,128)(2,1)} collective-permute-done((bf16[32,9216]{1,0:T(8,128)(2,1)S(1)}, bf16[32,9216]{1,0:T(8,128)(2,1)}, u32[]{:S(2)}, u32[]{:S(2)}) %collective-permute-start.13) | collective-permute-done | bytes 589856 | tf_op jit(solution)/shard_map/ppermute | solution.py:35
  272.0 8.2 %collective-permute-start.16 = (bf16[32,9216]{1,0:T(8,128)(2,1)}, bf16[32,9216]{1,0:T(8,128)(2,1)}, u32[]{:S(2)}, u32[]{:S(2)}) collective-permute-start(bf16[32,9216]{1,0:T(8,128)(2,1)} %get-tuple-element.65), channel_id=1, source_target_pairs={{0,1},{1,2},{2,3},{4,5},{5,6},{6,7},{8,9},{9,10},{10,11},{12,13},{... | collective-permute-start | bytes 1769480 | tf_op jit(solution)/shard_map/ppermute | solution.py:35
  282.7 7.4 %collective-permute-done.16 = bf16[32,9216]{1,0:T(8,128)(2,1)} collective-permute-done((bf16[32,9216]{1,0:T(8,128)(2,1)}, bf16[32,9216]{1,0:T(8,128)(2,1)}, u32[]{:S(2)}, u32[]{:S(2)}) %collective-permute-start.16) | collective-permute-done | bytes 589856 | tf_op jit(solution)/shard_map/ppermute | solution.py:35
  300.8 8.2 %collective-permute-done.18 = bf16[32,9216]{1,0:T(8,128)(2,1)S(1)} collective-permute-done((bf16[32,9216]{1,0:T(8,128)(2,1)S(1)}, bf16[32,9216]{1,0:T(8,128)(2,1)S(1)}, u32[]{:S(2)}, u32[]{:S(2)}) %collective-permute-start.18) | collective-permute-done | bytes 589856 | tf_op jit(solution)/shard_map/ppermute | solution.py:53
  317.1 12.5 %collective-permute-done.22 = bf16[32,9216]{1,0:T(8,128)(2,1)} collective-permute-done((bf16[32,9216]{1,0:T(8,128)(2,1)S(1)}, bf16[32,9216]{1,0:T(8,128)(2,1)}, u32[]{:S(2)}, u32[]{:S(2)}) %collective-permute-start.22) | collective-permute-done | bytes 589856 | tf_op jit(solution)/shard_map/ppermute | solution.py:54
  330.9 12.4 %collective-permute-done.23 = bf16[32,9216]{1,0:T(8,128)(2,1)} collective-permute-done((bf16[32,9216]{1,0:T(8,128)(2,1)}, bf16[32,9216]{1,0:T(8,128)(2,1)}, u32[]{:S(2)}, u32[]{:S(2)}) %collective-permute-start.23) | collective-permute-done | bytes 589856 | tf_op jit(solution)/shard_map/ppermute | solution.py:54
  361.4 7.5 %collective-permute-done.25 = bf16[32,9216]{1,0:T(8,128)(2,1)S(1)} collective-permute-done((bf16[32,9216]{1,0:T(8,128)(2,1)S(1)}, bf16[32,9216]{1,0:T(8,128)(2,1)S(1)}, u32[]{:S(2)}, u32[]{:S(2)}) %collective-permute-start.25) | collective-permute-done | bytes 589856 | tf_op jit(solution)/shard_map/ppermute | solution.py:54
  370.9 11.4 %collective-permute-done.26 = bf16[32,9216]{1,0:T(8,128)(2,1)S(1)} collective-permute-done((bf16[32,9216]{1,0:T(8,128)(2,1)S(1)}, bf16[32,9216]{1,0:T(8,128)(2,1)S(1)}, u32[]{:S(2)}, u32[]{:S(2)}) %collective-permute-start.26) | collective-permute-done | bytes 589856 | tf_op jit(solution)/shard_map/ppermute | solution.py:54
  384.4 9.8 %collective-permute-done.27 = bf16[32,9216]{1,0:T(8,128)(2,1)S(1)} collective-permute-done((bf16[32,9216]{1,0:T(8,128)(2,1)S(1)}, bf16[32,9216]{1,0:T(8,128)(2,1)S(1)}, u32[]{:S(2)}, u32[]{:S(2)}) %collective-permute-start.27) | collective-permute-done | bytes 589856 | tf_op jit(solution)/shard_map/ppermute | solution.py:54
  401.0 23.3 %collective-permute-done.30 = bf16[4,32,6144]{2,1,0:T(8,128)(2,1)} collective-permute-done((bf16[4,32,6144]{2,1,0:T(8,128)(2,1)S(1)}, bf16[4,32,6144]{2,1,0:T(8,128)(2,1)}, u32[]{:S(2)}, u32[]{:S(2)}) %collective-permute-start.30) | collective-permute-done | bytes 1572896 | tf_op jit(solution)/shard_map/ppermute | solution.py:53
  429.6 15.3 %all-gather.5.cloned.1.call-done = bf16[512,9216]{1,0:T(8,128)(2,1)} async-done(((bf16[128,9216]{1,0:T(8,128)(2,1)}), bf16[512,9216]{1,0:T(8,128)(2,1)}) %all-gather.5.cloned.1.call-update) | async-done | bytes 9437200 | tf_op jit(solution)/shard_map/all_gather | solution.py:142
  449.8 33.1 %collective-permute-done.32 = bf16[4,32,6144]{2,1,0:T(8,128)(2,1)S(1)} collective-permute-done((bf16[4,32,6144]{2,1,0:T(8,128)(2,1)S(1)}, bf16[4,32,6144]{2,1,0:T(8,128)(2,1)S(1)}, u32[]{:S(2)}, u32[]{:S(2)}) %collective-permute-start.32) | collective-permute-done | bytes 1572896 | tf_op jit(solution)/shard_map/ppermute | solution.py:54
  490.3 8.3 %fusion.1 = f32[512,384]{1,0:T(8,128)S(1)} fusion(bf16[512,9216]{1,0:T(8,128)(2,1)S(1)} %copy-done.3, bf16[384,12288]{1,0:T(8,128)(2,1)} %param.6), kind=kOutput, calls=%fused_computation.8 | convolution fusion | flops 3623878656 | bytes 17301504 | tf_op jit(solution)/shard_map/dot_general | solution.py:154
  499.6 20.7 %collective-permute-done.33 = bf16[4,32,6144]{2,1,0:T(8,128)(2,1)} collective-permute-done((bf16[4,32,6144]{2,1,0:T(8,128)(2,1)S(1)}, bf16[4,32,6144]{2,1,0:T(8,128)(2,1)}, u32[]{:S(2)}, u32[]{:S(2)}) %collective-permute-start.33) | collective-permute-done | bytes 1572896 | tf_op jit(solution)/shard_map/ppermute | solution.py:54
  547.2 8.1 %convolution_convert_fusion.2 = bf16[384,9216]{1,0:T(8,128)(2,1)S(1)} fusion(bf16[512,384]{1,0:T(8,128)(2,1)S(1)} %bitcast.130, bf16[512,9216]{1,0:T(8,128)(2,1)} %all-gather.7.cloned.1.call-done), kind=kOutput, calls=%fused_computation.2 | convolution fusion | flops 3627417600 | bytes 16908288 | tf_op jit(solution)/shard_map/dot_general | solution.py:97
  (153 shorter events, 201.3 us)
Async XLA Ops:
  7.2 125.1 %reduce-scatter.4.cloned.1.call-start = ((), (), s32[]{:S(2)}) async-start(), calls=%async_computation.5 | async-start | bytes 11796480 | tf_op jit(solution)/shard_map/reduce_scatter | solution.py:106
  37.7 193.3 %reduce-scatter.6.cloned.1.call-start = ((), (), s32[]{:S(2)}) async-start(), calls=%async_computation.6 | async-start | bytes 11796480 | tf_op jit(solution)/shard_map/reduce_scatter | solution.py:114
  52.6 36.8 %collective-permute-start = (bf16[4,32,6144]{2,1,0:T(8,128)(2,1)}, bf16[4,32,6144]{2,1,0:T(8,128)(2,1)S(1)}, u32[]{:S(2)}, u32[]{:S(2)}) collective-permute-start(bf16[4,32,6144]{2,1,0:T(8,128)(2,1)} %get-tuple-element.64), channel_id=1, source_target_pairs={{0,1},{4,5},{8,9},{12,13},{16,17},{20,21},{24,25},{28,29}} | collective-permute-start | bytes 4718600 | tf_op jit(solution)/shard_map/ppermute | solution.py:35
  56.2 33.2 %collective-permute-start.2 = (bf16[4,32,6144]{2,1,0:T(8,128)(2,1)}, bf16[4,32,6144]{2,1,0:T(8,128)(2,1)}, u32[]{:S(2)}, u32[]{:S(2)}) collective-permute-start(bf16[4,32,6144]{2,1,0:T(8,128)(2,1)} %get-tuple-element.63), channel_id=1, source_target_pairs={{3,2},{7,6},{11,10},{15,14},{19,18},{23,22},{27,26},{31,30}} | collective-permute-start | bytes 4718600 | tf_op jit(solution)/shard_map/ppermute | solution.py:36
  93.7 36.8 %collective-permute-start.1 = (bf16[4,32,6144]{2,1,0:T(8,128)(2,1)}, bf16[4,32,6144]{2,1,0:T(8,128)(2,1)S(1)}, u32[]{:S(2)}, u32[]{:S(2)}) collective-permute-start(bf16[4,32,6144]{2,1,0:T(8,128)(2,1)} %get-tuple-element.62), channel_id=1, source_target_pairs={{0,1},{1,2},{4,5},{5,6},{8,9},{9,10},{12,13},{13,14},{16,17},{17,1... | collective-permute-start | bytes 4718600 | tf_op jit(solution)/shard_map/ppermute | solution.py:35
  98.2 32.3 %collective-permute-start.3 = (bf16[4,32,6144]{2,1,0:T(8,128)(2,1)}, bf16[4,32,6144]{2,1,0:T(8,128)(2,1)}, u32[]{:S(2)}, u32[]{:S(2)}) collective-permute-start(bf16[4,32,6144]{2,1,0:T(8,128)(2,1)} %get-tuple-element.61), channel_id=1, source_target_pairs={{2,1},{3,2},{6,5},{7,6},{10,9},{11,10},{14,13},{15,14},{18,17},{19... | collective-permute-start | bytes 4718600 | tf_op jit(solution)/shard_map/ppermute | solution.py:36
  132.3 136.9 %reduce-scatter.8.cloned.1.call-start = ((), (), s32[]{:S(2)}) async-start(), calls=%async_computation.7 | async-start | bytes 1966080 | tf_op jit(solution)/shard_map/reduce_scatter | solution.py:121
  135.6 16.7 %collective-permute-start.6 = (bf16[32,9216]{1,0:T(8,128)(2,1)}, bf16[32,9216]{1,0:T(8,128)(2,1)}, u32[]{:S(2)}, u32[]{:S(2)}) collective-permute-start(bf16[32,9216]{1,0:T(8,128)(2,1)} %get-tuple-element.74), channel_id=1, source_target_pairs={{0,1},{4,5},{8,9},{12,13},{16,17},{20,21},{24,25},{28,29}} | collective-permute-start | bytes 1769480 | tf_op jit(solution)/shard_map/ppermute | solution.py:35
  153.8 32.2 %collective-permute-start.7 = (bf16[32,9216]{1,0:T(8,128)(2,1)S(1)}, bf16[32,9216]{1,0:T(8,128)(2,1)S(1)}, u32[]{:S(2)}, u32[]{:S(2)}) collective-permute-start(bf16[32,9216]{1,0:T(8,128)(2,1)S(1)} %get-tuple-element.72), channel_id=1, source_target_pairs={{0,1},{1,2},{4,5},{5,6},{8,9},{9,10},{12,13},{13,14},{16,17},{17,1... | collective-permute-start | bytes 1769480 | tf_op jit(solution)/shard_map/ppermute | solution.py:35
  175.1 44.6 %collective-permute-start.4 = (bf16[4,32,6144]{2,1,0:T(8,128)(2,1)S(1)}, bf16[4,32,6144]{2,1,0:T(8,128)(2,1)S(1)}, u32[]{:S(2)}, u32[]{:S(2)}) collective-permute-start(bf16[4,32,6144]{2,1,0:T(8,128)(2,1)S(1)} %get-tuple-element.59), channel_id=1, source_target_pairs={{0,1},{1,2},{2,3},{4,5},{5,6},{6,7},{8,9},{9,10},{10,11},{12,13},{... | collective-permute-start | bytes 4718600 | tf_op jit(solution)/shard_map/ppermute | solution.py:35
  179.0 40.7 %collective-permute-start.5 = (bf16[4,32,6144]{2,1,0:T(8,128)(2,1)S(1)}, bf16[4,32,6144]{2,1,0:T(8,128)(2,1)S(1)}, u32[]{:S(2)}, u32[]{:S(2)}) collective-permute-start(bf16[4,32,6144]{2,1,0:T(8,128)(2,1)S(1)} %get-tuple-element.60), channel_id=1, source_target_pairs={{1,0},{2,1},{3,2},{5,4},{6,5},{7,6},{9,8},{10,9},{11,10},{13,12},{... | collective-permute-start | bytes 4718600 | tf_op jit(solution)/shard_map/ppermute | solution.py:36
  180.3 45.7 %collective-permute-start.11 = (bf16[32,9216]{1,0:T(8,128)(2,1)S(1)}, bf16[32,9216]{1,0:T(8,128)(2,1)}, u32[]{:S(2)}, u32[]{:S(2)}) collective-permute-start(bf16[32,9216]{1,0:T(8,128)(2,1)S(1)} %get-tuple-element.71), channel_id=1, source_target_pairs={{1,0},{2,1},{3,2},{5,4},{6,5},{7,6},{9,8},{10,9},{11,10},{13,12},{... | collective-permute-start | bytes 1769480 | tf_op jit(solution)/shard_map/ppermute | solution.py:36
  186.1 42.3 %collective-permute-start.8 = (bf16[32,9216]{1,0:T(8,128)(2,1)S(1)}, bf16[32,9216]{1,0:T(8,128)(2,1)}, u32[]{:S(2)}, u32[]{:S(2)}) collective-permute-start(bf16[32,9216]{1,0:T(8,128)(2,1)S(1)} %bitcast_add_fusion.11), channel_id=1, source_target_pairs={{0,1},{1,2},{2,3},{4,5},{5,6},{6,7},{8,9},{9,10},{10,11},{12,13},{... | collective-permute-start | bytes 1769480 | tf_op jit(solution)/shard_map/ppermute | solution.py:35
  239.1 104.2 %all-gather.9.cloned.1.call-start = ((), (), s32[]{:S(2)}) async-start(), calls=%async_computation.10 | async-start | bytes 1966080 | tf_op jit(solution)/shard_map/all_gather | solution.py:133
  272.0 18.1 %collective-permute-start.16 = (bf16[32,9216]{1,0:T(8,128)(2,1)}, bf16[32,9216]{1,0:T(8,128)(2,1)}, u32[]{:S(2)}, u32[]{:S(2)}) collective-permute-start(bf16[32,9216]{1,0:T(8,128)(2,1)} %get-tuple-element.65), channel_id=1, source_target_pairs={{0,1},{1,2},{2,3},{4,5},{5,6},{6,7},{8,9},{9,10},{10,11},{12,13},{... | collective-permute-start | bytes 1769480 | tf_op jit(solution)/shard_map/ppermute | solution.py:35
  282.6 162.3 %all-gather.5.cloned.1.call-start = ((), (), s32[]{:S(2)}) async-start(), calls=%async_computation.8 | async-start | bytes 11796480 | tf_op jit(solution)/shard_map/all_gather | solution.py:142
  350.9 196.3 %all-gather.7.cloned.1.call-start = ((), (), s32[]{:S(2)}) async-start(), calls=%async_computation.9 | async-start | bytes 11796480 | tf_op jit(solution)/shard_map/all_gather | solution.py:148
  383.7 16.4 %collective-permute-start.29 = (bf16[32,9216]{1,0:T(8,128)(2,1)S(1)}, bf16[32,9216]{1,0:T(8,128)(2,1)S(1)}, u32[]{:S(2)}, u32[]{:S(2)}) collective-permute-start(bf16[32,9216]{1,0:T(8,128)(2,1)S(1)} %collective-permute-done.28), channel_id=1, source_target_pairs={{2,3},{6,7},{10,11},{14,15},{18,19},{22,23},{26,27},{30,31}} | collective-permute-start | bytes 1769480 | tf_op jit(solution)/shard_map/ppermute | solution.py:53
  396.0 28.3 %collective-permute-start.30 = (bf16[4,32,6144]{2,1,0:T(8,128)(2,1)S(1)}, bf16[4,32,6144]{2,1,0:T(8,128)(2,1)}, u32[]{:S(2)}, u32[]{:S(2)}) collective-permute-start(bf16[4,32,6144]{2,1,0:T(8,128)(2,1)S(1)} %bitcast.137), channel_id=1, source_target_pairs={{0,1},{1,2},{2,3},{4,5},{5,6},{6,7},{8,9},{9,10},{10,11},{12,13},{... | collective-permute-start | bytes 4718600 | tf_op jit(solution)/shard_map/ppermute | solution.py:53
  398.7 30.9 %collective-permute-start.31 = (bf16[4,32,6144]{2,1,0:T(8,128)(2,1)S(1)}, bf16[4,32,6144]{2,1,0:T(8,128)(2,1)S(1)}, u32[]{:S(2)}, u32[]{:S(2)}) collective-permute-start(bf16[4,32,6144]{2,1,0:T(8,128)(2,1)S(1)} %bitcast.138), channel_id=1, source_target_pairs={{1,0},{2,1},{3,2},{5,4},{6,5},{7,6},{9,8},{10,9},{11,10},{13,12},{... | collective-permute-start | bytes 4718600 | tf_op jit(solution)/shard_map/ppermute | solution.py:54
  444.9 38.0 %collective-permute-start.32 = (bf16[4,32,6144]{2,1,0:T(8,128)(2,1)S(1)}, bf16[4,32,6144]{2,1,0:T(8,128)(2,1)S(1)}, u32[]{:S(2)}, u32[]{:S(2)}) collective-permute-start(bf16[4,32,6144]{2,1,0:T(8,128)(2,1)S(1)} %collective-permute-done.31), channel_id=1, source_target_pairs={{1,0},{2,1},{5,4},{6,5},{9,8},{10,9},{13,12},{14,13},{17,16},{18,1... | collective-permute-start | bytes 4718600 | tf_op jit(solution)/shard_map/ppermute | solution.py:54
  448.9 49.7 %collective-permute-start.34 = (bf16[4,32,6144]{2,1,0:T(8,128)(2,1)}, bf16[4,32,6144]{2,1,0:T(8,128)(2,1)S(1)}, u32[]{:S(2)}, u32[]{:S(2)}) collective-permute-start(bf16[4,32,6144]{2,1,0:T(8,128)(2,1)} %collective-permute-done.30), channel_id=1, source_target_pairs={{1,2},{2,3},{5,6},{6,7},{9,10},{10,11},{13,14},{14,15},{17,18},{18... | collective-permute-start | bytes 4718600 | tf_op jit(solution)/shard_map/ppermute | solution.py:53
  482.9 37.4 %collective-permute-start.33 = (bf16[4,32,6144]{2,1,0:T(8,128)(2,1)S(1)}, bf16[4,32,6144]{2,1,0:T(8,128)(2,1)}, u32[]{:S(2)}, u32[]{:S(2)}) collective-permute-start(bf16[4,32,6144]{2,1,0:T(8,128)(2,1)S(1)} %collective-permute-done.32), channel_id=1, source_target_pairs={{1,0},{5,4},{9,8},{13,12},{17,16},{21,20},{25,24},{29,28}} | collective-permute-start | bytes 4718600 | tf_op jit(solution)/shard_map/ppermute | solution.py:54
  498.6 24.2 %collective-permute-start.35 = (bf16[4,32,6144]{2,1,0:T(8,128)(2,1)S(1)}, bf16[4,32,6144]{2,1,0:T(8,128)(2,1)S(1)}, u32[]{:S(2)}, u32[]{:S(2)}) collective-permute-start(bf16[4,32,6144]{2,1,0:T(8,128)(2,1)S(1)} %collective-permute-done.34), channel_id=1, source_target_pairs={{2,3},{6,7},{10,11},{14,15},{18,19},{22,23},{26,27},{30,31}} | collective-permute-start | bytes 4718600 | tf_op jit(solution)/shard_map/ppermute | solution.py:53
  (35 other events, 424.5 us)
Sparse Core Ops, SparseCore 0:
  37.8 94.4 reduce-scatter.3
  136.0 94.9 reduce-scatter.5
  239.2 29.9 reduce-scatter.7
  282.8 30.2 all-gather.8
  351.0 93.8 all-gather.4
  446.6 100.5 all-gather.6

commit v3 on v2

--- a/solution.py
+++ b/solution.py
@@ -118,12 +118,13 @@
     pre_move = line_sums(pre_near, 0, "col", steps)
     grad_near, far_sum, pre_move = tie((grad_near, far_sum, pre_move))
 
+    near_value, near_slope = gelu_parts(line_total(pre_near, 0, "col", pre_move))
+    act_near = near_value.astype(bf16)
     far_sum = lax.psum_scatter(
         far_sum.reshape(n_depth * bunch, 2 * far), "depth", scatter_dimension=0, tiled=True
     )
-    grad_near = grad_near.reshape(n_col, bunch, near)
-    grad_move = line_sums(grad_near, 0, "col", steps[:-third])
-    far_sum, grad_move = tie((far_sum, grad_move))
+    act_move = line_moves(act_near, "col", steps[:-third])
+    far_sum, act_move = tie((far_sum, act_move))
 
     far_sum = far_sum.astype(f32)
     far_value, far_slope = gelu_parts(far_sum[:, :far])
@@ -131,21 +132,21 @@
         [far_value.astype(bf16), (far_sum[:, far:] * far_slope).astype(bf16)], axis=1
     )
     far_pair = lax.all_gather(far_pair, "depth", axis=0, tiled=False)
-    grad_move = line_sums(grad_near, 0, "col", steps[-third:], grad_move)
-    near_value, near_slope = gelu_parts(line_total(pre_near, 0, "col", pre_move))
-    act_near = near_value.astype(bf16)
+    act_move = line_moves(act_near, "col", steps[-third:], act_move)
+    act_near = line_whole(act_near, 0, "col", act_move).reshape(n_col * bunch, near)
+    grad_near = grad_near.reshape(n_col, bunch, near)
+    grad_move = line_sums(grad_near, 0, "col", steps[:third])
+    far_pair, act_near, grad_move = tie((far_pair, act_near, grad_move))
+
+    act_near = lax.all_gather(act_near, "depth", axis=0, tiled=True)
+    grad_move = line_sums(grad_near, 0, "col", steps[third:], grad_move)
     hid_near = (line_total(grad_near, 0, "col", grad_move) * near_slope).astype(bf16)
     hid_move = line_moves(hid_near, "col", steps)
-    far_pair, hid_near, hid_move = tie((far_pair, hid_near, hid_move))
+    hid_near = line_whole(hid_near, 0, "col", hid_move).reshape(n_col * bunch, near)
+    far_move = line_moves(far_pair, "col", steps[:third])
+    act_near, hid_near, far_move = tie((act_near, hid_near, far_move))
 
-    hid_near = line_whole(hid_near, 0, "col", hid_move).reshape(n_col * bunch, near)
     hid_near = lax.all_gather(hid_near, "depth", axis=0, tiled=True)
-    act_move = line_moves(act_near, "col", steps)
-    act_near = line_whole(act_near, 0, "col", act_move).reshape(n_col * bunch, near)
-    far_move = line_moves(far_pair, "col", steps[:third])
-    hid_near, act_near, far_move = tie((hid_near, act_near, far_move))
-
-    act_near = lax.all_gather(act_near, "depth", axis=0, tiled=True)
     far_move = line_moves(far_pair, "col", steps[third:], far_move)
     far_pair = line_whole(far_pair, 1, "col", far_move).reshape(total, 2 * far)
     act_far, hid_far = far_pair[:, :far], far_pair[:, far:]
@@ -155,15 +156,18 @@
             left, right, (((1,), (1,)), ((), ())), preferred_element_type=f32
         )
 
-    grad_in = back(hid_near, w_up[:, :near]) + back(hid_far, w_up[:, near:])
-    grad_in = grad_in.astype(bf16).reshape(group, rows, narrow)
+    grad_down = jnp.concatenate([outer(dy_cols, act_near), outer(dy_cols, act_far)], axis=1)
+    up_far = outer(x_cols, hid_far)
+    in_far = back(hid_far, w_up[:, near:])
+    hid_near, grad_down, up_far, in_far = tie((hid_near, grad_down, up_far, in_far))
+
+    grad_in = (back(hid_near, w_up[:, :near]) + in_far).astype(bf16)
+    grad_in, hid_near = tie((grad_in, hid_near))
+    grad_in = grad_in.reshape(group, rows, narrow)
     grad_in = lax.all_to_all(grad_in, ("depth", "row"), 0, 0, tiled=True)
     grad_in = grad_in.reshape(n_depth, n_row, rows, narrow).astype(f32).sum(axis=1)
     grad_in = jnp.transpose(grad_in, (1, 0, 2)).reshape(rows, part).astype(bf16)
-    grad_up = jnp.concatenate([outer(x_cols, hid_near), outer(x_cols, hid_far)], axis=1)
-    down_far = outer(dy_cols, act_far)
-    act_near, grad_in, grad_up, down_far = tie((act_near, grad_in, grad_up, down_far))
-    grad_down = jnp.concatenate([outer(dy_cols, act_near), down_far], axis=1)
+    grad_up = jnp.concatenate([outer(x_cols, hid_near), up_far], axis=1)
     return (grad_in, grad_up, grad_down)
 
 

time: 574 us -> 578 us (level); the launches traced: 566 us -> 576 us
  waiting for transfers between devices: 298 us -> 312 us
    all_gather x1, waiting for transfers between devices: 0.01 us -> 14.8 us  [body(): far_pair = lax.all_gather(far_pair, 'depth', axis=0, tiled=False)]
    ppermute x9, waiting for transfers between devices: 8.01 us -> 17.8 us  [line_sums(): lax.ppermute(send_down, name, [(i, i - 1) for i in range(count - step, co...]
    ppermute x9, waiting for transfers between devices: 31.6 us -> 25 us  [line_moves(): lax.ppermute(up, name, [(i, i + 1) for i in range(step - 1, count - 1)])]
    add x7 -> x8, other arithmetic: 14.2 us -> 13.5 us  [line_sums(): send_up, send_down = (send_up + carry[0], send_down + carry[1])]
  transfers between devices with their start and end apart: 43 -> 43, of which waited for: 28 -> 26; matrix products, arithmetic and copies ran while one was open for 16% -> 16% of each run, Pallas kernels for 0% -> 0%
where the time goes in v3:
time: 578 us; the launch traced here: 576 us
  waiting for transfers between devices  312 us (54%)
  starting transfers between devices  106 us (18%)
  matrix products  60.6 us (10%)
  other arithmetic  49.4 us (9%)
  blocking collectives  17.5 us (3%)
  local copies, waits for them, and re-layouts  16.7 us (3%)
  between operations  14.6 us (3%)
    ppermute x9, waiting for transfers between devices, line_sums(): lax.ppermute(send_up, name, [(i, i + 1) for i in range(step)])  116 us
    ppermute x9, waiting for transfers between devices, line_moves(): lax.ppermute(down, name, [(i, i - 1) for i in range(1, count - step + 1)])  114 us
    ppermute x9, starting transfers between devices, line_sums(): lax.ppermute(send_up, name, [(i, i + 1) for i in range(step)])  57.9 us
    dot_general x4, matrix products, product(): return jnp.dot(left, right, preferred_element_type=f32).astype(bf16)  29.5 us
    ppermute x9, waiting for transfers between devices, line_moves(): lax.ppermute(up, name, [(i, i + 1) for i in range(step - 1, count - 1)])  25 us
    ppermute x9, starting transfers between devices, line_moves(): lax.ppermute(up, name, [(i, i + 1) for i in range(step - 1, count - 1)])  20.7 us
    all_gather x1, waiting for transfers between devices, body(): hid_near = lax.all_gather(hid_near, 'depth', axis=0, tiled=True)  19.6 us
    ppermute x9, waiting for transfers between devices, line_sums(): lax.ppermute(send_down, name, [(i, i - 1) for i in range(count - step, co...  17.8 us
  transfers between devices with their start and end apart: 43, of which 26 were waited for; matrix products, arithmetic and copies ran while one was open for 16% of the time, Pallas kernels for 0%

profile of v3, /device:TPU:0, one launch (start us, length us, event | category | flops | bytes accessed | tf_op | source)
XLA Modules:
  0.0 576.3 jit_solution(15363979690699781839)
XLA Ops:
  9.6 17.5 %all_to_all.10 = bf16[8,2,64,384]{3,2,1,0:T(8,128)(2,1)S(1)} all-to-all(bf16[8,2,64,384]{3,2,1,0:T(8,128)(2,1)S(1)} %bitcast.136), channel_id=1, replica_groups=mesh['depth'=4,'row'=2,'col'=4] {'depth','row'}, dimensions={0} | all-to-all | bytes 1572864 | tf_op jit(solution)/shard_map/all_to_all | solution.py:89
  27.2 10.5 %convolution_convert_fusion.1 = bf16[512,9216]{1,0:T(8,128)(2,1)} fusion(bf16[512,384]{1,0:T(8,128)(2,1)S(1)} %bitcast.128, bf16[384,12288]{1,0:T(8,128)(2,1)} %param.6), kind=kOutput, calls=%fused_computation.1 | convolution fusion | flops 3628597248 | bytes 16908288 | tf_op jit(solution)/shard_map/dot_general | solution.py:94
  58.0 31.4 %collective-permute-done = bf16[4,32,6144]{2,1,0:T(8,128)(2,1)S(1)} collective-permute-done((bf16[4,32,6144]{2,1,0:T(8,128)(2,1)}, bf16[4,32,6144]{2,1,0:T(8,128)(2,1)S(1)}, u32[]{:S(2)}, u32[]{:S(2)}) %collective-permute-start) | collective-permute-done | bytes 1572896 | tf_op jit(solution)/shard_map/ppermute | solution.py:35
  100.0 10.4 %convolution_convert_fusion = bf16[512,9216]{1,0:T(8,128)(2,1)} fusion(bf16[512,384]{1,0:T(8,128)(2,1)S(1)} %bitcast.133, bf16[384,12288]{1,0:T(8,128)(2,1)} %param.7), kind=kOutput, calls=%fused_computation | convolution fusion | flops 3628597248 | bytes 16908288 | tf_op jit(solution)/shard_map/dot_general | solution.py:94
  110.4 20.0 %collective-permute-done.1 = bf16[4,32,6144]{2,1,0:T(8,128)(2,1)S(1)} collective-permute-done((bf16[4,32,6144]{2,1,0:T(8,128)(2,1)}, bf16[4,32,6144]{2,1,0:T(8,128)(2,1)S(1)}, u32[]{:S(2)}, u32[]{:S(2)}) %collective-permute-start.1) | collective-permute-done | bytes 1572896 | tf_op jit(solution)/shard_map/ppermute | solution.py:35
  135.5 7.4 %collective-permute-start.6 = (bf16[32,9216]{1,0:T(8,128)(2,1)}, bf16[32,9216]{1,0:T(8,128)(2,1)}, u32[]{:S(2)}, u32[]{:S(2)}) collective-permute-start(bf16[32,9216]{1,0:T(8,128)(2,1)} %get-tuple-element.74), channel_id=1, source_target_pairs={{0,1},{4,5},{8,9},{12,13},{16,17},{20,21},{24,25},{28,29}} | collective-permute-start | bytes 1769480 | tf_op jit(solution)/shard_map/ppermute | solution.py:35
  153.7 18.7 %collective-permute-start.7 = (bf16[32,9216]{1,0:T(8,128)(2,1)S(1)}, bf16[32,9216]{1,0:T(8,128)(2,1)S(1)}, u32[]{:S(2)}, u32[]{:S(2)}) collective-permute-start(bf16[32,9216]{1,0:T(8,128)(2,1)S(1)} %get-tuple-element.72), channel_id=1, source_target_pairs={{0,1},{1,2},{4,5},{5,6},{8,9},{9,10},{12,13},{13,14},{16,17},{17,1... | collective-permute-start | bytes 1769480 | tf_op jit(solution)/shard_map/ppermute | solution.py:35
  191.4 28.4 %collective-permute-done.4 = bf16[4,32,6144]{2,1,0:T(8,128)(2,1)S(1)} collective-permute-done((bf16[4,32,6144]{2,1,0:T(8,128)(2,1)S(1)}, bf16[4,32,6144]{2,1,0:T(8,128)(2,1)S(1)}, u32[]{:S(2)}, u32[]{:S(2)}) %collective-permute-start.4) | collective-permute-done | bytes 1572896 | tf_op jit(solution)/shard_map/ppermute | solution.py:35
  241.1 10.7 %collective-permute-done.12 = bf16[32,9216]{1,0:T(8,128)(2,1)} collective-permute-done((bf16[32,9216]{1,0:T(8,128)(2,1)}, bf16[32,9216]{1,0:T(8,128)(2,1)}, u32[]{:S(2)}, u32[]{:S(2)}) %collective-permute-start.12) | collective-permute-done | bytes 589856 | tf_op jit(solution)/shard_map/ppermute | solution.py:53
  277.8 10.3 %collective-permute-done.16 = bf16[32,9216]{1,0:T(8,128)(2,1)} collective-permute-done((bf16[32,9216]{1,0:T(8,128)(2,1)}, bf16[32,9216]{1,0:T(8,128)(2,1)}, u32[]{:S(2)}, u32[]{:S(2)}) %collective-permute-start.16) | collective-permute-done | bytes 589856 | tf_op jit(solution)/shard_map/ppermute | solution.py:54
  294.2 14.8 %all-gather.9.cloned.1.call-done = bf16[128,6144]{1,0:T(8,128)(2,1)} async-done(((bf16[32,6144]{1,0:T(8,128)(2,1)}), bf16[128,6144]{1,0:T(8,128)(2,1)}) %all-gather.9.cloned.1.call-update) | async-done | bytes 1572880 | tf_op jit(solution)/shard_map/all_gather | solution.py:134
  315.4 12.0 %collective-permute-done.20 = bf16[32,9216]{1,0:T(8,128)(2,1)} collective-permute-done((bf16[32,9216]{1,0:T(8,128)(2,1)}, bf16[32,9216]{1,0:T(8,128)(2,1)}, u32[]{:S(2)}, u32[]{:S(2)}) %collective-permute-start.20) | collective-permute-done | bytes 589856 | tf_op jit(solution)/shard_map/ppermute | solution.py:35
  336.2 10.3 %collective-permute-done.21 = bf16[32,9216]{1,0:T(8,128)(2,1)S(1)} collective-permute-done((bf16[32,9216]{1,0:T(8,128)(2,1)S(1)}, bf16[32,9216]{1,0:T(8,128)(2,1)S(1)}, u32[]{:S(2)}, u32[]{:S(2)}) %collective-permute-start.21) | collective-permute-done | bytes 589856 | tf_op jit(solution)/shard_map/ppermute | solution.py:35
  346.5 14.8 %collective-permute-done.23 = bf16[32,9216]{1,0:T(8,128)(2,1)S(1)} collective-permute-done((bf16[32,9216]{1,0:T(8,128)(2,1)S(1)}, bf16[32,9216]{1,0:T(8,128)(2,1)S(1)}, u32[]{:S(2)}, u32[]{:S(2)}) %collective-permute-start.23) | collective-permute-done | bytes 589856 | tf_op jit(solution)/shard_map/ppermute | solution.py:36
  372.1 8.7 %collective-permute-done.25 = bf16[32,9216]{1,0:T(8,128)(2,1)S(1)} collective-permute-done((bf16[32,9216]{1,0:T(8,128)(2,1)S(1)}, bf16[32,9216]{1,0:T(8,128)(2,1)S(1)}, u32[]{:S(2)}, u32[]{:S(2)}) %collective-permute-start.25) | collective-permute-done | bytes 589856 | tf_op jit(solution)/shard_map/ppermute | solution.py:54
  382.8 11.8 %collective-permute-done.26 = bf16[32,9216]{1,0:T(8,128)(2,1)S(1)} collective-permute-done((bf16[32,9216]{1,0:T(8,128)(2,1)S(1)}, bf16[32,9216]{1,0:T(8,128)(2,1)S(1)}, u32[]{:S(2)}, u32[]{:S(2)}) %collective-permute-start.26) | collective-permute-done | bytes 589856 | tf_op jit(solution)/shard_map/ppermute | solution.py:54
  403.7 9.1 %collective-permute-done.27 = bf16[32,9216]{1,0:T(8,128)(2,1)S(1)} collective-permute-done((bf16[32,9216]{1,0:T(8,128)(2,1)S(1)}, bf16[32,9216]{1,0:T(8,128)(2,1)S(1)}, u32[]{:S(2)}, u32[]{:S(2)}) %collective-permute-start.27) | collective-permute-done | bytes 589856 | tf_op jit(solution)/shard_map/ppermute | solution.py:54
  415.7 14.3 %collective-permute-done.30 = bf16[4,32,6144]{2,1,0:T(8,128)(2,1)} collective-permute-done((bf16[4,32,6144]{2,1,0:T(8,128)(2,1)S(1)}, bf16[4,32,6144]{2,1,0:T(8,128)(2,1)}, u32[]{:S(2)}, u32[]{:S(2)}) %collective-permute-start.30) | collective-permute-done | bytes 1572896 | tf_op jit(solution)/shard_map/ppermute | solution.py:53
  429.9 11.7 %collective-permute-done.31 = bf16[4,32,6144]{2,1,0:T(8,128)(2,1)S(1)} collective-permute-done((bf16[4,32,6144]{2,1,0:T(8,128)(2,1)S(1)}, bf16[4,32,6144]{2,1,0:T(8,128)(2,1)S(1)}, u32[]{:S(2)}, u32[]{:S(2)}) %collective-permute-start.31) | collective-permute-done | bytes 1572896 | tf_op jit(solution)/shard_map/ppermute | solution.py:54
  443.9 31.4 %collective-permute-done.32 = bf16[4,32,6144]{2,1,0:T(8,128)(2,1)S(1)} collective-permute-done((bf16[4,32,6144]{2,1,0:T(8,128)(2,1)S(1)}, bf16[4,32,6144]{2,1,0:T(8,128)(2,1)S(1)}, u32[]{:S(2)}, u32[]{:S(2)}) %collective-permute-start.32) | collective-permute-done | bytes 1572896 | tf_op jit(solution)/shard_map/ppermute | solution.py:54
  477.5 8.1 %convolution_convert_fusion.3 = bf16[384,9216]{1,0:T(8,128)(2,1)S(1)} fusion(bf16[512,384]{1,0:T(8,128)(2,1)S(1)} %bitcast.134, bf16[512,9216]{1,0:T(8,128)(2,1)} %all-gather.5.cloned.1.call-done), kind=kOutput, calls=%fused_computation.3 | convolution fusion | flops 3627417600 | bytes 16908288 | tf_op jit(solution)/shard_map/dot_general | solution.py:97
  486.6 22.1 %collective-permute-done.33 = bf16[4,32,6144]{2,1,0:T(8,128)(2,1)S(1)} collective-permute-done((bf16[4,32,6144]{2,1,0:T(8,128)(2,1)S(1)}, bf16[4,32,6144]{2,1,0:T(8,128)(2,1)S(1)}, u32[]{:S(2)}, u32[]{:S(2)}) %collective-permute-start.33) | collective-permute-done | bytes 1572896 | tf_op jit(solution)/shard_map/ppermute | solution.py:54
  520.7 19.6 %all-gather.7.cloned.1.call-done = bf16[512,9216]{1,0:T(8,128)(2,1)} async-done(((bf16[128,9216]{1,0:T(8,128)(2,1)}), bf16[512,9216]{1,0:T(8,128)(2,1)}) %all-gather.7.cloned.1.call-update) | async-done | bytes 9437200 | tf_op jit(solution)/shard_map/all_gather | solution.py:149
  540.3 10.6 %fusion.16 = bf16[512,384]{1,0:T(8,128)(2,1)} fusion(f32[512,384]{1,0:T(8,128)S(1)} %fusion.7, bf16[512,9216]{1,0:T(8,128)(2,1)} %all-gather.7.cloned.1.call-done, bf16[384,12288]{1,0:T(8,128)(2,1)} %param.6), kind=kOutput, calls=%fused_computation.38 | convolution fusion | flops 3624271872 | bytes 17694720 | tf_op jit(solution)/shard_map/dot_general | solution.py:155
  (136 shorter events, 197.2 us)
Async XLA Ops:
  7.2 125.1 %reduce-scatter.4.cloned.1.call-start = ((), (), s32[]{:S(2)}) async-start(), calls=%async_computation.5 | async-start | bytes 11796480 | tf_op jit(solution)/shard_map/reduce_scatter | solution.py:106
  37.7 193.3 %reduce-scatter.6.cloned.1.call-start = ((), (), s32[]{:S(2)}) async-start(), calls=%async_computation.6 | async-start | bytes 11796480 | tf_op jit(solution)/shard_map/reduce_scatter | solution.py:114
  52.6 36.8 %collective-permute-start = (bf16[4,32,6144]{2,1,0:T(8,128)(2,1)}, bf16[4,32,6144]{2,1,0:T(8,128)(2,1)S(1)}, u32[]{:S(2)}, u32[]{:S(2)}) collective-permute-start(bf16[4,32,6144]{2,1,0:T(8,128)(2,1)} %get-tuple-element.66), channel_id=1, source_target_pairs={{0,1},{4,5},{8,9},{12,13},{16,17},{20,21},{24,25},{28,29}} | collective-permute-start | bytes 4718600 | tf_op jit(solution)/shard_map/ppermute | solution.py:35
  56.1 33.2 %collective-permute-start.2 = (bf16[4,32,6144]{2,1,0:T(8,128)(2,1)}, bf16[4,32,6144]{2,1,0:T(8,128)(2,1)}, u32[]{:S(2)}, u32[]{:S(2)}) collective-permute-start(bf16[4,32,6144]{2,1,0:T(8,128)(2,1)} %get-tuple-element.65), channel_id=1, source_target_pairs={{3,2},{7,6},{11,10},{15,14},{19,18},{23,22},{27,26},{31,30}} | collective-permute-start | bytes 4718600 | tf_op jit(solution)/shard_map/ppermute | solution.py:36
  93.7 36.8 %collective-permute-start.1 = (bf16[4,32,6144]{2,1,0:T(8,128)(2,1)}, bf16[4,32,6144]{2,1,0:T(8,128)(2,1)S(1)}, u32[]{:S(2)}, u32[]{:S(2)}) collective-permute-start(bf16[4,32,6144]{2,1,0:T(8,128)(2,1)} %get-tuple-element.64), channel_id=1, source_target_pairs={{0,1},{1,2},{4,5},{5,6},{8,9},{9,10},{12,13},{13,14},{16,17},{17,1... | collective-permute-start | bytes 4718600 | tf_op jit(solution)/shard_map/ppermute | solution.py:35
  98.1 32.3 %collective-permute-start.3 = (bf16[4,32,6144]{2,1,0:T(8,128)(2,1)}, bf16[4,32,6144]{2,1,0:T(8,128)(2,1)}, u32[]{:S(2)}, u32[]{:S(2)}) collective-permute-start(bf16[4,32,6144]{2,1,0:T(8,128)(2,1)} %get-tuple-element.63), channel_id=1, source_target_pairs={{2,1},{3,2},{6,5},{7,6},{10,9},{11,10},{14,13},{15,14},{18,17},{19... | collective-permute-start | bytes 4718600 | tf_op jit(solution)/shard_map/ppermute | solution.py:36
  132.3 140.6 %reduce-scatter.8.cloned.1.call-start = ((), (), s32[]{:S(2)}) async-start(), calls=%async_computation.7 | async-start | bytes 1966080 | tf_op jit(solution)/shard_map/reduce_scatter | solution.py:123
  153.7 32.4 %collective-permute-start.7 = (bf16[32,9216]{1,0:T(8,128)(2,1)S(1)}, bf16[32,9216]{1,0:T(8,128)(2,1)S(1)}, u32[]{:S(2)}, u32[]{:S(2)}) collective-permute-start(bf16[32,9216]{1,0:T(8,128)(2,1)S(1)} %get-tuple-element.72), channel_id=1, source_target_pairs={{0,1},{1,2},{4,5},{5,6},{8,9},{9,10},{12,13},{13,14},{16,17},{17,1... | collective-permute-start | bytes 1769480 | tf_op jit(solution)/shard_map/ppermute | solution.py:35
  175.2 44.6 %collective-permute-start.4 = (bf16[4,32,6144]{2,1,0:T(8,128)(2,1)S(1)}, bf16[4,32,6144]{2,1,0:T(8,128)(2,1)S(1)}, u32[]{:S(2)}, u32[]{:S(2)}) collective-permute-start(bf16[4,32,6144]{2,1,0:T(8,128)(2,1)S(1)} %get-tuple-element.61), channel_id=1, source_target_pairs={{0,1},{1,2},{2,3},{4,5},{5,6},{6,7},{8,9},{9,10},{10,11},{12,13},{... | collective-permute-start | bytes 4718600 | tf_op jit(solution)/shard_map/ppermute | solution.py:35
  179.1 40.7 %collective-permute-start.5 = (bf16[4,32,6144]{2,1,0:T(8,128)(2,1)S(1)}, bf16[4,32,6144]{2,1,0:T(8,128)(2,1)S(1)}, u32[]{:S(2)}, u32[]{:S(2)}) collective-permute-start(bf16[4,32,6144]{2,1,0:T(8,128)(2,1)S(1)} %get-tuple-element.62), channel_id=1, source_target_pairs={{1,0},{2,1},{3,2},{5,4},{6,5},{7,6},{9,8},{10,9},{11,10},{13,12},{... | collective-permute-start | bytes 4718600 | tf_op jit(solution)/shard_map/ppermute | solution.py:36
  180.4 45.7 %collective-permute-start.11 = (bf16[32,9216]{1,0:T(8,128)(2,1)S(1)}, bf16[32,9216]{1,0:T(8,128)(2,1)}, u32[]{:S(2)}, u32[]{:S(2)}) collective-permute-start(bf16[32,9216]{1,0:T(8,128)(2,1)S(1)} %get-tuple-element.71), channel_id=1, source_target_pairs={{1,0},{2,1},{3,2},{5,4},{6,5},{7,6},{9,8},{10,9},{11,10},{13,12},{... | collective-permute-start | bytes 1769480 | tf_op jit(solution)/shard_map/ppermute | solution.py:36
  186.2 42.3 %collective-permute-start.8 = (bf16[32,9216]{1,0:T(8,128)(2,1)S(1)}, bf16[32,9216]{1,0:T(8,128)(2,1)}, u32[]{:S(2)}, u32[]{:S(2)}) collective-permute-start(bf16[32,9216]{1,0:T(8,128)(2,1)S(1)} %bitcast_add_fusion.11), channel_id=1, source_target_pairs={{0,1},{1,2},{2,3},{4,5},{5,6},{6,7},{8,9},{9,10},{10,11},{12,13},{... | collective-permute-start | bytes 1769480 | tf_op jit(solution)/shard_map/ppermute | solution.py:35
  231.1 77.9 %all-gather.9.cloned.1.call-start = ((), (), s32[]{:S(2)}) async-start(), calls=%async_computation.10 | async-start | bytes 1966080 | tf_op jit(solution)/shard_map/all_gather | solution.py:134
  260.4 33.8 %collective-permute-start.18 = (bf16[32,9216]{1,0:T(8,128)(2,1)}, bf16[32,9216]{1,0:T(8,128)(2,1)}, u32[]{:S(2)}, u32[]{:S(2)}) collective-permute-start(bf16[32,9216]{1,0:T(8,128)(2,1)} %get-tuple-element.70), channel_id=1, source_target_pairs={{0,1},{4,5},{8,9},{12,13},{16,17},{20,21},{24,25},{28,29}} | collective-permute-start | bytes 1769480 | tf_op jit(solution)/shard_map/ppermute | solution.py:35
  265.8 28.4 %collective-permute-start.19 = (bf16[32,9216]{1,0:T(8,128)(2,1)}, bf16[32,9216]{1,0:T(8,128)(2,1)}, u32[]{:S(2)}, u32[]{:S(2)}) collective-permute-start(bf16[32,9216]{1,0:T(8,128)(2,1)} %get-tuple-element.69), channel_id=1, source_target_pairs={{3,2},{7,6},{11,10},{15,14},{19,18},{23,22},{27,26},{31,30}} | collective-permute-start | bytes 1769480 | tf_op jit(solution)/shard_map/ppermute | solution.py:36
  277.8 163.9 %all-gather.5.cloned.1.call-start = ((), (), s32[]{:S(2)}) async-start(), calls=%async_computation.8 | async-start | bytes 11796480 | tf_op jit(solution)/shard_map/all_gather | solution.py:141
  315.4 224.9 %all-gather.7.cloned.1.call-start = ((), (), s32[]{:S(2)}) async-start(), calls=%async_computation.9 | async-start | bytes 11796480 | tf_op jit(solution)/shard_map/all_gather | solution.py:149
  334.9 26.4 %collective-permute-start.23 = (bf16[32,9216]{1,0:T(8,128)(2,1)S(1)}, bf16[32,9216]{1,0:T(8,128)(2,1)S(1)}, u32[]{:S(2)}, u32[]{:S(2)}) collective-permute-start(bf16[32,9216]{1,0:T(8,128)(2,1)S(1)} %bitcast_add_fusion.5), channel_id=1, source_target_pairs={{1,0},{2,1},{3,2},{5,4},{6,5},{7,6},{9,8},{10,9},{11,10},{13,12},{... | collective-permute-start | bytes 1769480 | tf_op jit(solution)/shard_map/ppermute | solution.py:36
  395.9 34.0 %collective-permute-start.30 = (bf16[4,32,6144]{2,1,0:T(8,128)(2,1)S(1)}, bf16[4,32,6144]{2,1,0:T(8,128)(2,1)}, u32[]{:S(2)}, u32[]{:S(2)}) collective-permute-start(bf16[4,32,6144]{2,1,0:T(8,128)(2,1)S(1)} %bitcast.137), channel_id=1, source_target_pairs={{0,1},{1,2},{2,3},{4,5},{5,6},{6,7},{8,9},{9,10},{10,11},{12,13},{... | collective-permute-start | bytes 4718600 | tf_op jit(solution)/shard_map/ppermute | solution.py:53
  401.7 40.0 %collective-permute-start.31 = (bf16[4,32,6144]{2,1,0:T(8,128)(2,1)S(1)}, bf16[4,32,6144]{2,1,0:T(8,128)(2,1)S(1)}, u32[]{:S(2)}, u32[]{:S(2)}) collective-permute-start(bf16[4,32,6144]{2,1,0:T(8,128)(2,1)S(1)} %bitcast.138), channel_id=1, source_target_pairs={{1,0},{2,1},{3,2},{5,4},{6,5},{7,6},{9,8},{10,9},{11,10},{13,12},{... | collective-permute-start | bytes 4718600 | tf_op jit(solution)/shard_map/ppermute | solution.py:54
  441.7 33.6 %collective-permute-start.32 = (bf16[4,32,6144]{2,1,0:T(8,128)(2,1)S(1)}, bf16[4,32,6144]{2,1,0:T(8,128)(2,1)S(1)}, u32[]{:S(2)}, u32[]{:S(2)}) collective-permute-start(bf16[4,32,6144]{2,1,0:T(8,128)(2,1)S(1)} %collective-permute-done.31), channel_id=1, source_target_pairs={{1,0},{2,1},{5,4},{6,5},{9,8},{10,9},{13,12},{14,13},{17,16},{18,1... | collective-permute-start | bytes 4718600 | tf_op jit(solution)/shard_map/ppermute | solution.py:54
  443.1 42.5 %collective-permute-start.34 = (bf16[4,32,6144]{2,1,0:T(8,128)(2,1)}, bf16[4,32,6144]{2,1,0:T(8,128)(2,1)S(1)}, u32[]{:S(2)}, u32[]{:S(2)}) collective-permute-start(bf16[4,32,6144]{2,1,0:T(8,128)(2,1)} %collective-permute-done.30), channel_id=1, source_target_pairs={{1,2},{2,3},{5,6},{6,7},{9,10},{10,11},{13,14},{14,15},{17,18},{18... | collective-permute-start | bytes 4718600 | tf_op jit(solution)/shard_map/ppermute | solution.py:53
  475.3 33.4 %collective-permute-start.33 = (bf16[4,32,6144]{2,1,0:T(8,128)(2,1)S(1)}, bf16[4,32,6144]{2,1,0:T(8,128)(2,1)S(1)}, u32[]{:S(2)}, u32[]{:S(2)}) collective-permute-start(bf16[4,32,6144]{2,1,0:T(8,128)(2,1)S(1)} %collective-permute-done.32), channel_id=1, source_target_pairs={{1,0},{5,4},{9,8},{13,12},{17,16},{21,20},{25,24},{29,28}} | collective-permute-start | bytes 4718600 | tf_op jit(solution)/shard_map/ppermute | solution.py:54
  485.6 24.2 %collective-permute-start.35 = (bf16[4,32,6144]{2,1,0:T(8,128)(2,1)S(1)}, bf16[4,32,6144]{2,1,0:T(8,128)(2,1)S(1)}, u32[]{:S(2)}, u32[]{:S(2)}) collective-permute-start(bf16[4,32,6144]{2,1,0:T(8,128)(2,1)S(1)} %collective-permute-done.34), channel_id=1, source_target_pairs={{2,3},{6,7},{10,11},{14,15},{18,19},{22,23},{26,27},{30,31}} | collective-permute-start | bytes 4718600 | tf_op jit(solution)/shard_map/ppermute | solution.py:53
  (27 other events, 407.5 us)
Sparse Core Ops, SparseCore 0:
  37.8 94.3 reduce-scatter.3
  136.0 95.0 reduce-scatter.5
  234.0 30.9 reduce-scatter.7
  277.9 31.0 all-gather.8
  315.5 93.6 all-gather.4
  441.8 98.4 all-gather.6
